TPU v7x, 256 devices: a whole 4x4x8 slice. The times are simulated.
256 devices in a mesh: section: 4 (over x), replica: 64 (over y, z, core).
Axes of the slice: x: 4, y: 4, z: 8, core: 2. Of those that a mesh axis runs over, the one named last changes fastest.
Arguments:
- hidden_in: bfloat16 [2, 4096, 4096], P(None, 'replica'), may hold values from -16 to 16
- down_weight: bfloat16 [4, 4096, 128], P('section'), may hold values from -0.09375 to 0.09375
- up_weight: bfloat16 [4, 4096, 128], P('section'), may hold values from -0.5 to 0.5
- norm_gain: float32 [4, 4096], P('section'), may hold values from 0.1 to 1.9
- krylov_basis: float32 [6, 4, 2, 4096, 128], P(None, 'section', None, 'replica'), may hold values from -60 to 60, as said below
Outputs:
- new_vectors: float32 [2, 4, 2, 4096, 128], P(None, 'section', None, 'replica')
- hessenberg: float32 [2, 9], replicated
Inputs may be any that keep to these rules, and one draw needn't show every extreme that they name: `krylov_basis`: krylov basis vectors, one per leading index.
All inputs are finite; a program needn't handle non-finite values.
Results may differ from a plain program's by a relative error of at most 0.00085.
Values may be sent and summed in bfloat16 or wider, within the bound.
A program may use at most 64 MiB of HBM per device.

v0:
```python
import jax
import jax.numpy as jnp
from jax import lax
from jax.sharding import PartitionSpec as P

ITERS = 2


NORM_EPS = 1e-05
VEC_EPS = 1e-06


def shifted(block, axis, distance):
    devices = range(lax.axis_size(axis))
    route = [(i - distance, i) for i in devices if i - distance in devices]
    return lax.ppermute(block, axis, route)


def primal_parts(rows_in, down_rows, gain_row):
    widened = rows_in.astype(jnp.float32)
    inv_rms = lax.rsqrt(jnp.mean(widened * widened, axis=-1, keepdims=True) + NORM_EPS)
    normed = (widened * inv_rms * gain_row).astype(jnp.bfloat16)
    pre_act = jnp.dot(normed, down_rows, preferred_element_type=jnp.float32)
    sig_val = jax.nn.sigmoid(pre_act)
    return (widened, inv_rms, normed, pre_act, sig_val)


def against_rows(left, right):
    return lax.dot_general(
        left, right, (((1,), (1,)), ((), ())), preferred_element_type=jnp.float32
    )


def over_tokens(left, right):
    return lax.dot_general(
        left, right, (((0,), (0,)), ((), ())), preferred_element_type=jnp.float32
    )


def tangent_part(
    widened,
    inv_rms,
    normed,
    pre_act,
    sig_val,
    hidden_act,
    tangent_in,
    down_rows,
    up_rows,
    gain_row,
    tan_down,
    tan_up,
):
    wide_tan = tangent_in.astype(jnp.float32)
    tan_rms = -(inv_rms * inv_rms * inv_rms) * jnp.mean(widened * wide_tan, axis=-1, keepdims=True)
    tan_normed = ((wide_tan * inv_rms + widened * tan_rms) * gain_row).astype(jnp.bfloat16)
    tan_pre = jnp.dot(tan_normed, down_rows, preferred_element_type=jnp.float32) + jnp.dot(
        normed, tan_down, preferred_element_type=jnp.float32
    )
    sig_slope = sig_val + pre_act * sig_val * (1.0 - sig_val)
    tan_act = (tan_pre * sig_slope).astype(jnp.bfloat16)
    return (wide_tan + against_rows(tan_act, up_rows) + against_rows(hidden_act, tan_up)).astype(
        jnp.bfloat16
    )


def backward_pieces(rows_in, cotangent, down_rows, up_rows, gain_row):
    widened, inv_rms, normed, pre_act, sig_val = primal_parts(rows_in, down_rows, gain_row)
    hidden_act = (pre_act * sig_val).astype(jnp.bfloat16)
    back_act = jnp.dot(cotangent, up_rows, preferred_element_type=jnp.float32)
    sig_slope = sig_val + pre_act * sig_val * (1.0 - sig_val)
    back_pre = (back_act * sig_slope).astype(jnp.bfloat16)
    back_norm = against_rows(back_pre, down_rows) * gain_row
    cube = inv_rms * inv_rms * inv_rms
    back_rows = (
        cotangent.astype(jnp.float32)
        + inv_rms * back_norm
        - widened * cube * jnp.mean(back_norm * widened, axis=-1, keepdims=True)
    )
    return (back_rows.astype(jnp.bfloat16), normed, hidden_act, back_pre)


def store_block(buffer, piece, micro_slot, is_valid):
    current = lax.dynamic_index_in_dim(buffer, micro_slot, 0, keepdims=False)
    return lax.dynamic_update_index_in_dim(
        buffer, jnp.where(is_valid, piece, current), micro_slot, 0
    )


def curvature_product(hidden_in, down_weight, up_weight, norm_gain, vector):
    full_d = down_weight.shape[1]
    rank = down_weight.shape[2]
    scales = jnp.array([full_d ** (-0.5), rank ** (-0.5)], dtype=jnp.float32).reshape(1, 2, 1, 1)
    tangent_shard = (vector * scales).astype(jnp.bfloat16)
    tangent_full = lax.all_gather(tangent_shard, "replica", axis=2, tiled=True)
    tan_down = tangent_full[0, 0]
    tan_up = tangent_full[0, 1]
    down_rows = down_weight[0]
    up_rows = up_weight[0]
    gain_row = norm_gain[0]
    section_pos = lax.axis_index("section")
    section_count = lax.axis_size("section")
    micro_count = hidden_in.shape[0]
    tok_rows = hidden_in.shape[1]
    turn_count = micro_count + section_count - 1
    at_first = section_pos == 0
    at_final = section_pos == section_count - 1
    blank_rows = jnp.zeros((tok_rows, full_d), jnp.bfloat16)
    tan_store = jnp.zeros(hidden_in.shape, jnp.bfloat16)
    inputs = jnp.zeros(hidden_in.shape, jnp.bfloat16)
    recv_rows = blank_rows
    recv_tan = blank_rows
    for turn_idx in range(turn_count):
        micro_idx = turn_idx - section_pos
        is_valid = (micro_idx >= 0) & (micro_idx < micro_count)
        micro_slot = jnp.clip(micro_idx, 0, micro_count - 1)
        own_rows = lax.dynamic_index_in_dim(hidden_in, micro_slot, 0, keepdims=False)
        rows_in = jnp.where(at_first, own_rows, recv_rows)
        tangent_in = jnp.where(at_first, blank_rows, recv_tan)
        widened, inv_rms, normed, pre_act, sig_val = primal_parts(rows_in, down_rows, gain_row)
        hidden_act = (pre_act * sig_val).astype(jnp.bfloat16)
        result = (widened + against_rows(hidden_act, up_rows)).astype(jnp.bfloat16)
        tangent_out = tangent_part(
            widened,
            inv_rms,
            normed,
            pre_act,
            sig_val,
            hidden_act,
            tangent_in,
            down_rows,
            up_rows,
            gain_row,
            tan_down,
            tan_up,
        )
        inputs = store_block(inputs, rows_in, micro_slot, is_valid)
        tan_store = store_block(tan_store, tangent_out, micro_slot, is_valid)
        if turn_idx + 1 < turn_count:
            recv_rows, recv_tan = shifted((result, tangent_out), "section", 1)
    cot_store = jnp.zeros(hidden_in.shape, jnp.bfloat16)
    normed_store = jnp.zeros(hidden_in.shape, jnp.bfloat16)
    act_store = jnp.zeros((micro_count, tok_rows, rank), jnp.bfloat16)
    pre_store = jnp.zeros((micro_count, tok_rows, rank), jnp.bfloat16)
    recv_back = blank_rows
    for turn_idx in range(turn_count):
        micro_idx = turn_idx - (section_count - 1 - section_pos)
        is_valid = (micro_idx >= 0) & (micro_idx < micro_count)
        micro_slot = jnp.clip(micro_idx, 0, micro_count - 1)
        rows_in = lax.dynamic_index_in_dim(inputs, micro_slot, 0, keepdims=False)
        last_tan = lax.dynamic_index_in_dim(tan_store, micro_slot, 0, keepdims=False)
        cotangent = jnp.where(at_final, last_tan, recv_back)
        back_rows, normed, hidden_act, back_pre = backward_pieces(
            rows_in, cotangent, down_rows, up_rows, gain_row
        )
        cot_store = store_block(cot_store, cotangent, micro_slot, is_valid)
        normed_store = store_block(normed_store, normed, micro_slot, is_valid)
        act_store = store_block(act_store, hidden_act, micro_slot, is_valid)
        pre_store = store_block(pre_store, back_pre, micro_slot, is_valid)
        if turn_idx + 1 < turn_count:
            recv_back = shifted(back_rows, "section", -1)
    all_rows = micro_count * tok_rows
    grad_up = over_tokens(cot_store.reshape(all_rows, full_d), act_store.reshape(all_rows, rank))
    grad_down = over_tokens(
        normed_store.reshape(all_rows, full_d), pre_store.reshape(all_rows, rank)
    )
    norm_factor = 1.0 / (micro_count * tok_rows * lax.axis_size("replica"))
    term_sum = jnp.stack(
        [grad_down * (full_d ** (-0.5) * norm_factor), grad_up * (rank ** (-0.5) * norm_factor)]
    )[None]
    return lax.psum_scatter(term_sum, "replica", scatter_dimension=2, tiled=True)


def local_correlations(slot_bank, vector):
    return jnp.sum(slot_bank * vector[None], axis=(1, 2, 3, 4))


def combine(coef, slot_bank):
    return jnp.tensordot(coef, slot_bank, axes=1, precision=lax.Precision.HIGHEST)


def per_device(hidden_in, down_weight, up_weight, norm_gain, krylov_basis):
    base_count = krylov_basis.shape[0]
    slot_bank = jnp.concatenate(
        [krylov_basis, jnp.zeros((ITERS,) + krylov_basis.shape[1:], jnp.float32)], axis=0
    )
    param_count = float(lax.axis_size("section") * 2 * down_weight.shape[1] * down_weight.shape[2])
    hess_rows = []
    for iter_idx in range(ITERS):
        image = curvature_product(
            hidden_in, down_weight, up_weight, norm_gain, slot_bank[base_count - 1 + iter_idx]
        )
        first_coef = (
            lax.psum(local_correlations(slot_bank, image), ("section", "replica")) / param_count
        )
        cleaned = image - combine(first_coef, slot_bank)
        second_coef = (
            lax.psum(local_correlations(slot_bank, cleaned), ("section", "replica")) / param_count
        )
        twice_clean = cleaned - combine(second_coef, slot_bank)
        square_mean = (
            lax.psum(jnp.sum(twice_clean * twice_clean), ("section", "replica")) / param_count
        )
        length = jnp.sqrt(square_mean + VEC_EPS)
        slot_bank = slot_bank.at[base_count + iter_idx].set(twice_clean / length)
        hess_rows.append(jnp.concatenate([first_coef + second_coef, length[None]]))
    return (slot_bank[base_count:], jnp.stack(hess_rows))


def solution(mesh):
    return jax.shard_map(
        per_device,
        mesh=mesh,
        in_specs=(
            P(None, "replica", None),
            P("section", None, None),
            P("section", None, None),
            P("section", None),
            P(None, "section", None, "replica", None),
        ),
        out_specs=(P(None, "section", None, "replica", None), P()),
        check_vma=False,
    )
```

profile of v0, /device:TPU:1, one launch (start us, length us, event | category | flops | bytes accessed | tf_op | source)
XLA Modules:
  0.0 1233.5 jit_solution(11115282961621367463)
XLA Ops:
  7.2 1.7 fusion.336
  10.4 1.8 fusion.258
  13.5 4.8 collective-permute-start
  19.7 73.3 %all-gather.3.cloned.1.call-done = bf16[1,2,4096,128]{3,2,1,0:T(8,128)(2,1)} async-done(((bf16[1,2,64,128]{3,2,1,0:T(8,128)(2,1)}), bf16[1,2,4096,128]{3,2,1,0:T(8,128)(2,1)}) %all-gather.3.cloned.1.call-update) | async-done | bytes 2097168 | tf_op jit(solution)/shard_map/all_gather | solution.py:95
  93.0 3.2 fusion.99
  96.2 2.1 bitcast_dynamic-update-slice_fusion.15
  98.4 3.1 collective-permute-start.4
  103.6 9.0 collective-permute-done.4
  115.1 4.9 collective-permute-start.1
  122.0 3.7 bitcast_dynamic-update-slice_fusion.14
  125.7 2.4 collective-permute-start.5
  128.0 1.9 constant_dynamic-slice_fusion.25
  131.4 9.6 collective-permute-done.5
  143.5 4.8 collective-permute-start.2
  150.2 3.6 bitcast_dynamic-update-slice_fusion.13
  153.9 2.6 collective-permute-start.6
  156.5 1.9 constant_dynamic-slice_fusion.24
  158.7 9.8 collective-permute-done.6
  171.0 4.8 collective-permute-start.3
  177.8 3.6 bitcast_dynamic-update-slice_fusion.12
  181.4 2.4 collective-permute-start.7
  183.9 1.9 constant_dynamic-slice_fusion.23
  188.2 7.6 collective-permute-done.7
  199.7 3.4 fusion.33
  209.3 9.8 collective-permute-done.8
  222.4 10.0 collective-permute-done.9
  235.4 9.4 collective-permute-done.10
  246.4 1.5 collective-permute-start.11
  248.0 8.3 collective-permute-done.11
  257.9 2.3 maximum_bitcast_fusion
  260.3 141.9 %reduce-scatter.3.cloned.1.call-done = f32[1,2,64,128]{3,2,1,0:T(8,128)} async-done(((f32[1,2,4096,128]{3,2,1,0:T(8,128)}), f32[1,2,64,128]{3,2,1,0:T(8,128)}) %reduce-scatter.3.cloned.1.call-update) | async-done | bytes 65552 | tf_op jit(solution)/shard_map/reduce_scatter | solution.py:171
  402.1 2.2 multiply_reduce_fusion.3
  404.3 79.4 %psum.42 = f32[8]{0:T(128)} all-reduce(f32[8]{0:T(128)} %get-tuple-element.66), channel_id=1, replica_groups=mesh['section'=4,'replica'=64] {'section','replica'}, use_global_device_ids=true, to_apply=%region_21.22 | all-reduce | flops 8 | bytes 64 | tf_op jit(solution)/shard_map/psum | solution.py:194
  483.8 1.9 fusion.319
  488.0 73.6 %psum.43 = f32[8]{0:T(128)S(1)} all-reduce(f32[8]{0:T(128)} %get-tuple-element.64), channel_id=1, replica_groups=mesh['section'=4,'replica'=64] {'section','replica'}, use_global_device_ids=true, to_apply=%region_23.24 | all-reduce | flops 8 | bytes 64 | tf_op jit(solution)/shard_map/psum | solution.py:198
  561.5 1.8 fusion.317
  564.9 73.5 %psum.44 = f32[]{:T(128)} all-reduce(f32[]{:T(128)} %get-tuple-element.48), channel_id=1, replica_groups=mesh['section'=4,'replica'=64] {'section','replica'}, use_global_device_ids=true, to_apply=%region_25.26 | all-reduce | flops 1 | bytes 8 | tf_op jit(solution)/shard_map/psum | solution.py:202
  640.5 74.3 %all-gather.5.cloned.1.call-done = bf16[1,2,4096,128]{3,2,1,0:T(8,128)(2,1)} async-done(((bf16[1,2,64,128]{3,2,1,0:T(8,128)(2,1)}), bf16[1,2,4096,128]{3,2,1,0:T(8,128)(2,1)}) %all-gather.5.cloned.1.call-update) | async-done | bytes 2097168 | tf_op jit(solution)/shard_map/all_gather | solution.py:95
  714.7 3.2 fusion.95
  718.0 2.2 bitcast_dynamic-update-slice_fusion.7
  720.2 3.3 collective-permute-start.12
  725.8 8.7 collective-permute-done.12
  735.8 3.6 bitcast_dynamic-update-slice_fusion.6
  739.5 4.4 collective-permute-start.13
  743.9 2.7 fusion.266
  747.5 6.8 collective-permute-done.13
  755.6 3.7 bitcast_dynamic-update-slice_fusion.5
  759.3 4.7 collective-permute-start.14
  764.0 2.7 fusion.265
  767.5 5.5 collective-permute-done.14
  774.3 3.7 bitcast_dynamic-update-slice_fusion.4
  778.0 4.3 collective-permute-start.15
  782.3 2.7 fusion.264
  785.9 5.0 collective-permute-done.15
  792.2 3.4 fusion.35
  799.7 11.0 collective-permute-done.16
  813.6 9.5 collective-permute-done.17
  826.1 8.6 collective-permute-done.18
  837.8 8.6 collective-permute-done.19
  848.0 2.3 maximum_bitcast_fusion.1
  851.3 142.6 %reduce-scatter.5.cloned.1.call-done = f32[1,2,64,128]{3,2,1,0:T(8,128)} async-done(((f32[1,2,4096,128]{3,2,1,0:T(8,128)}), f32[1,2,64,128]{3,2,1,0:T(8,128)}) %reduce-scatter.5.cloned.1.call-update) | async-done | bytes 65552 | tf_op jit(solution)/shard_map/reduce_scatter | solution.py:171
  994.9 79.7 %psum.45 = f32[8]{0:T(128)S(1)} all-reduce(f32[8]{0:T(128)S(1)} %multiply_reduce_fusion.1), channel_id=1, replica_groups=mesh['section'=4,'replica'=64] {'section','replica'}, use_global_device_ids=true, to_apply=%region_36.37 | all-reduce | flops 8 | bytes 64 | tf_op jit(solution)/shard_map/psum | solution.py:194
  1076.5 73.2 %psum.46 = f32[8]{0:T(128)S(1)} all-reduce(f32[8]{0:T(128)S(1)} %multiply_reduce_fusion), channel_id=1, replica_groups=mesh['section'=4,'replica'=64] {'section','replica'}, use_global_device_ids=true, to_apply=%region_38.39 | all-reduce | flops 8 | bytes 64 | tf_op jit(solution)/shard_map/psum | solution.py:198
  1151.2 73.6 %psum.47 = f32[]{:T(128)} all-reduce(f32[]{:T(128)} %get-tuple-element.40), channel_id=1, replica_groups=mesh['section'=4,'replica'=64] {'section','replica'}, use_global_device_ids=true, to_apply=%region_40.41 | all-reduce | flops 1 | bytes 8 | tf_op jit(solution)/shard_map/psum | solution.py:202
  (374 shorter events, 79.0 us)
Async XLA Ops:
  7.2 85.8 %all-gather.3.cloned.1.call-start = ((), (), s32[]{:S(2)}) async-start(), calls=%async_computation.2 | async-start | bytes 2129920 | tf_op jit(solution)/shard_map/all_gather | solution.py:95
  8.9 393.2 %reduce-scatter.3.cloned.1.call-start = ((), (), s32[]{:S(2)}) async-start(), calls=%async_computation.3 | async-start | bytes 4259840 | tf_op jit(solution)/shard_map/reduce_scatter | solution.py:171
  10.4 82.6 %copy-start.78 = (f32[64]{0:T(128)}, f32[64]{0:T(128)S(1)}, u32[]{:S(2)}) copy-start(f32[64]{0:T(128)S(1)} %get-tuple-element.84) | copy-start | bytes 772
  12.3 84.0 %copy-start.46 = (f32[64,128]{1,0:T(8,128)}, f32[64,128]{1,0:T(8,128)S(1)}, u32[]{:S(2)}) copy-start(f32[64,128]{1,0:T(8,128)S(1)} %fusion.258) | copy-start | bytes 98308
  13.5 88.8 %collective-permute-start = (bf16[64,4096]{1,0:T(8,128)(2,1)}, bf16[64,4096]{1,0:T(8,128)(2,1)}, u32[]{:S(2)}, u32[]{:S(2)}) collective-permute-start(bf16[64,4096]{1,0:T(8,128)(2,1)} %fusion.24), channel_id=1, source_target_pairs={{0,64},{64,128},{128,192},{1,65},{65,129},{129,193},{2,66},{66,130... | collective-permute-start | bytes 1572872 | tf_op jit(solution)/shard_map/ppermute | solution.py:16
  18.7 77.4 %copy-start.53 = (f32[64,128]{1,0:T(8,128)}, f32[64,128]{1,0:T(8,128)S(1)}, u32[]{:S(2)}) copy-start(f32[64,128]{1,0:T(8,128)S(1)} %fusion.250) | copy-start | bytes 98308
  98.4 14.2 %collective-permute-start.4 = (bf16[64,4096]{1,0:T(8,128)(2,1)S(1)}, bf16[64,4096]{1,0:T(8,128)(2,1)S(1)}, u32[]{:S(2)}, u32[]{:S(2)}) collective-permute-start(bf16[64,4096]{1,0:T(8,128)(2,1)S(1)} %get-tuple-element.88), channel_id=1, source_target_pairs={{0,64},{64,128},{128,192},{1,65},{65,129},{129,193},{2,66},{66,130... | collective-permute-start | bytes 1572872 | tf_op jit(solution)/shard_map/ppermute | solution.py:16
  102.6 18.9 %copy-start.16 = (bf16[64,4096]{1,0:T(8,128)(2,1)}, bf16[64,4096]{1,0:T(8,128)(2,1)S(1)}, u32[]{:S(2)}) copy-start(bf16[64,4096]{1,0:T(8,128)(2,1)S(1)} %get-tuple-element.63) | copy-start | bytes 1572868
  115.1 14.8 %collective-permute-start.1 = (bf16[64,4096]{1,0:T(8,128)(2,1)}, bf16[64,4096]{1,0:T(8,128)(2,1)}, u32[]{:S(2)}, u32[]{:S(2)}) collective-permute-start(bf16[64,4096]{1,0:T(8,128)(2,1)} %fusion.25), channel_id=1, source_target_pairs={{0,64},{64,128},{128,192},{1,65},{65,129},{129,193},{2,66},{66,130... | collective-permute-start | bytes 1572872 | tf_op jit(solution)/shard_map/ppermute | solution.py:16
  125.7 15.3 %collective-permute-start.5 = (bf16[64,4096]{1,0:T(8,128)(2,1)}, bf16[64,4096]{1,0:T(8,128)(2,1)S(1)}, u32[]{:S(2)}, u32[]{:S(2)}) collective-permute-start(bf16[64,4096]{1,0:T(8,128)(2,1)} %get-tuple-element.90), channel_id=1, source_target_pairs={{0,64},{64,128},{128,192},{1,65},{65,129},{129,193},{2,66},{66,130... | collective-permute-start | bytes 1572872 | tf_op jit(solution)/shard_map/ppermute | solution.py:16
  131.3 18.4 %copy-start.18 = (bf16[64,4096]{1,0:T(8,128)(2,1)}, bf16[64,4096]{1,0:T(8,128)(2,1)S(1)}, u32[]{:S(2)}) copy-start(bf16[64,4096]{1,0:T(8,128)(2,1)S(1)} %get-tuple-element.61) | copy-start | bytes 1572868
  143.5 15.0 %collective-permute-start.2 = (bf16[64,4096]{1,0:T(8,128)(2,1)}, bf16[64,4096]{1,0:T(8,128)(2,1)}, u32[]{:S(2)}, u32[]{:S(2)}) collective-permute-start(bf16[64,4096]{1,0:T(8,128)(2,1)} %fusion.26), channel_id=1, source_target_pairs={{0,64},{64,128},{128,192},{1,65},{65,129},{129,193},{2,66},{66,130... | collective-permute-start | bytes 1572872 | tf_op jit(solution)/shard_map/ppermute | solution.py:16
  153.9 14.7 %collective-permute-start.6 = (bf16[64,4096]{1,0:T(8,128)(2,1)}, bf16[64,4096]{1,0:T(8,128)(2,1)S(1)}, u32[]{:S(2)}, u32[]{:S(2)}) collective-permute-start(bf16[64,4096]{1,0:T(8,128)(2,1)} %get-tuple-element.92), channel_id=1, source_target_pairs={{0,64},{64,128},{128,192},{1,65},{65,129},{129,193},{2,66},{66,130... | collective-permute-start | bytes 1572872 | tf_op jit(solution)/shard_map/ppermute | solution.py:16
  158.7 18.6 %copy-start.20 = (bf16[64,4096]{1,0:T(8,128)(2,1)}, bf16[64,4096]{1,0:T(8,128)(2,1)S(1)}, u32[]{:S(2)}) copy-start(bf16[64,4096]{1,0:T(8,128)(2,1)S(1)} %get-tuple-element.59) | copy-start | bytes 1572868
  171.0 14.8 %collective-permute-start.3 = (bf16[64,4096]{1,0:T(8,128)(2,1)}, bf16[64,4096]{1,0:T(8,128)(2,1)}, u32[]{:S(2)}, u32[]{:S(2)}) collective-permute-start(bf16[64,4096]{1,0:T(8,128)(2,1)} %fusion.27), channel_id=1, source_target_pairs={{0,64},{64,128},{128,192},{1,65},{65,129},{129,193},{2,66},{66,130... | collective-permute-start | bytes 1572872 | tf_op jit(solution)/shard_map/ppermute | solution.py:16
  181.4 14.4 %collective-permute-start.7 = (bf16[64,4096]{1,0:T(8,128)(2,1)}, bf16[64,4096]{1,0:T(8,128)(2,1)S(1)}, u32[]{:S(2)}, u32[]{:S(2)}) collective-permute-start(bf16[64,4096]{1,0:T(8,128)(2,1)} %get-tuple-element.94), channel_id=1, source_target_pairs={{0,64},{64,128},{128,192},{1,65},{65,129},{129,193},{2,66},{66,130... | collective-permute-start | bytes 1572872 | tf_op jit(solution)/shard_map/ppermute | solution.py:16
  186.1 11.0 copy-start.27
  186.6 18.6 %copy-start.85 = (f32[64]{0:T(128)}, f32[64]{0:T(128)S(1)}, u32[]{:S(2)}) copy-start(f32[64]{0:T(128)S(1)} %get-tuple-element.74) | copy-start | bytes 772
  186.6 20.7 %copy-start.76 = (f32[64]{0:T(128)}, f32[64]{0:T(128)S(1)}, u32[]{:S(2)}) copy-start(f32[64]{0:T(128)S(1)} %get-tuple-element.75) | copy-start | bytes 772
  186.6 33.7 %copy-start.74 = (f32[64]{0:T(128)}, f32[64]{0:T(128)S(1)}, u32[]{:S(2)}) copy-start(f32[64]{0:T(128)S(1)} %get-tuple-element.73) | copy-start | bytes 772
  186.6 33.7 %copy-start.83 = (f32[64]{0:T(128)}, f32[64]{0:T(128)S(1)}, u32[]{:S(2)}) copy-start(f32[64]{0:T(128)S(1)} %get-tuple-element.72) | copy-start | bytes 772
  187.0 16.1 %copy-start.96 = (f32[64,128]{1,0:T(8,128)}, f32[64,128]{1,0:T(8,128)S(1)}, u32[]{:S(2)}) copy-start(f32[64,128]{1,0:T(8,128)S(1)} %get-tuple-element.104) | copy-start | bytes 98308
  187.4 31.9 %copy-start.58 = (f32[64,128]{1,0:T(8,128)}, f32[64,128]{1,0:T(8,128)S(1)}, u32[]{:S(2)}) copy-start(f32[64,128]{1,0:T(8,128)S(1)} %get-tuple-element.106) | copy-start | bytes 98308
  187.5 46.2 %copy-start.72 = (f32[64]{0:T(128)}, f32[64]{0:T(128)S(1)}, u32[]{:S(2)}) copy-start(f32[64]{0:T(128)S(1)} %get-tuple-element.71) | copy-start | bytes 772
  187.5 46.2 %copy-start.81 = (f32[64]{0:T(128)}, f32[64]{0:T(128)S(1)}, u32[]{:S(2)}) copy-start(f32[64]{0:T(128)S(1)} %get-tuple-element.70) | copy-start | bytes 772
  187.5 58.5 %copy-start.70 = (f32[64]{0:T(128)}, f32[64]{0:T(128)S(1)}, u32[]{:S(2)}) copy-start(f32[64]{0:T(128)S(1)} %get-tuple-element.69) | copy-start | bytes 772
  187.5 58.5 %copy-start.79 = (f32[64]{0:T(128)}, f32[64]{0:T(128)S(1)}, u32[]{:S(2)}) copy-start(f32[64]{0:T(128)S(1)} %get-tuple-element.68) | copy-start | bytes 772
  188.1 44.6 %copy-start.56 = (f32[64,128]{1,0:T(8,128)}, f32[64,128]{1,0:T(8,128)S(1)}, u32[]{:S(2)}) copy-start(f32[64,128]{1,0:T(8,128)S(1)} %get-tuple-element.108) | copy-start | bytes 98308
  205.6 13.5 %collective-permute-start.8 = (bf16[64,4096]{1,0:T(8,128)(2,1)S(1)}, bf16[64,4096]{1,0:T(8,128)(2,1)S(1)}, u32[]{:S(2)}, u32[]{:S(2)}) collective-permute-start(bf16[64,4096]{1,0:T(8,128)(2,1)S(1)} %fusion.113), channel_id=1, source_target_pairs={{64,0},{128,64},{192,128},{65,1},{129,65},{193,129},{66,2},{130,66... | collective-permute-start | bytes 1572872 | tf_op jit(solution)/shard_map/ppermute | solution.py:16
  208.6 36.5 %copy-start.60 = (f32[64,128]{1,0:T(8,128)}, f32[64,128]{1,0:T(8,128)S(1)}, u32[]{:S(2)}) copy-start(f32[64,128]{1,0:T(8,128)S(1)} %get-tuple-element.110) | copy-start | bytes 98308
  209.2 47.5 %copy-start.14 = (bf16[2,64,4096]{2,1,0:T(8,128)(2,1)}, bf16[2,64,4096]{2,1,0:T(8,128)(2,1)S(1)}, u32[]{:S(2)}) copy-start(bf16[2,64,4096]{2,1,0:T(8,128)(2,1)S(1)} %select_dynamic-update-slice_fusion.2) | copy-start | bytes 3145732
  220.7 11.7 collective-permute-start.9
  222.3 34.0 %copy-start.54 = (f32[64,128]{1,0:T(8,128)}, f32[64,128]{1,0:T(8,128)S(1)}, u32[]{:S(2)}) copy-start(f32[64,128]{1,0:T(8,128)S(1)} %get-tuple-element.112) | copy-start | bytes 98308
  234.0 10.8 collective-permute-start.10
  235.3 22.1 %copy-start.51 = (bf16[2,64,128]{2,1,0:T(8,128)(2,1)}, bf16[2,64,128]{2,1,0:T(8,128)(2,1)S(1)}, u32[]{:S(2)}) copy-start(bf16[2,64,128]{2,1,0:T(8,128)(2,1)S(1)} %constant_dynamic-update-slice_fusion.4) | copy-start | bytes 98308
  246.4 9.9 collective-permute-start.11
  260.2 141.9 %copy-start.39 = (f32[6,1,2,64,128]{4,3,2,1,0:T(8,128)S(1)}, f32[6,1,2,64,128]{4,3,2,1,0:T(8,128)}, u32[]{:S(2)}) copy-start(f32[6,1,2,64,128]{4,3,2,1,0:T(8,128)} %param.15) | copy-start | bytes 1179652
  260.2 454.5 %all-gather.5.cloned.1.call-start = ((), (), s32[]{:S(2)}) async-start(), calls=%async_computation.4 | async-start | bytes 2129920 | tf_op jit(solution)/shard_map/all_gather | solution.py:95
  640.4 77.6 %copy-start.47 = (f32[64,128]{1,0:T(8,128)S(1)}, f32[64,128]{1,0:T(8,128)}, u32[]{:S(2)}) copy-start(f32[64,128]{1,0:T(8,128)} %copy-done.46) | copy-start | bytes 98308
  640.4 353.5 %reduce-scatter.5.cloned.1.call-start = ((), (), s32[]{:S(2)}) async-start(), calls=%async_computation.5 | async-start | bytes 4259840 | tf_op jit(solution)/shard_map/reduce_scatter | solution.py:171
  720.2 14.6 %copy-start.7 = (bf16[2,64,4096]{2,1,0:T(8,128)(2,1)}, bf16[2,64,4096]{2,1,0:T(8,128)(2,1)S(1)}, u32[]{:S(2)}) copy-start(bf16[2,64,4096]{2,1,0:T(8,128)(2,1)S(1)} %get-tuple-element.121) | copy-start | bytes 3145732
  720.2 14.3 %copy-start.17 = (bf16[64,4096]{1,0:T(8,128)(2,1)S(1)}, bf16[64,4096]{1,0:T(8,128)(2,1)}, u32[]{:S(2)}) copy-start(bf16[64,4096]{1,0:T(8,128)(2,1)} %copy-done.16) | copy-start | bytes 1572868
  720.2 14.6 %copy-start.88 = (f32[64]{0:T(128)S(1)}, f32[64]{0:T(128)}, u32[]{:S(2)}) copy-start(f32[64]{0:T(128)} %copy-done.87) | copy-start | bytes 772
  720.2 15.2 %copy-start.65 = (f32[64]{0:T(128)S(1)}, f32[64]{0:T(128)}, u32[]{:S(2)}) copy-start(f32[64]{0:T(128)} %copy-done.64) | copy-start | bytes 772
  720.2 14.3 %collective-permute-start.12 = (bf16[64,4096]{1,0:T(8,128)(2,1)S(1)}, bf16[64,4096]{1,0:T(8,128)(2,1)S(1)}, u32[]{:S(2)}, u32[]{:S(2)}) collective-permute-start(bf16[64,4096]{1,0:T(8,128)(2,1)S(1)} %get-tuple-element.122), channel_id=1, source_target_pairs={{0,64},{64,128},{128,192},{1,65},{65,129},{129,193},{2,66},{66,130... | collective-permute-start | bytes 1572872 | tf_op jit(solution)/shard_map/ppermute | solution.py:16
  739.5 14.8 %copy-start.19 = (bf16[64,4096]{1,0:T(8,128)(2,1)S(1)}, bf16[64,4096]{1,0:T(8,128)(2,1)}, u32[]{:S(2)}) copy-start(bf16[64,4096]{1,0:T(8,128)(2,1)} %copy-done.18) | copy-start | bytes 1572868
  739.5 15.1 %copy-start.90 = (f32[64]{0:T(128)S(1)}, f32[64]{0:T(128)}, u32[]{:S(2)}) copy-start(f32[64]{0:T(128)} %copy-done.89) | copy-start | bytes 772
  739.5 15.6 %copy-start.67 = (f32[64]{0:T(128)S(1)}, f32[64]{0:T(128)}, u32[]{:S(2)}) copy-start(f32[64]{0:T(128)} %copy-done.66) | copy-start | bytes 772
  739.5 14.8 %collective-permute-start.13 = (bf16[64,4096]{1,0:T(8,128)(2,1)}, bf16[64,4096]{1,0:T(8,128)(2,1)S(1)}, u32[]{:S(2)}, u32[]{:S(2)}) collective-permute-start(bf16[64,4096]{1,0:T(8,128)(2,1)} %get-tuple-element.124), channel_id=1, source_target_pairs={{0,64},{64,128},{128,192},{1,65},{65,129},{129,193},{2,66},{66,130... | collective-permute-start | bytes 1572872 | tf_op jit(solution)/shard_map/ppermute | solution.py:16
  759.3 13.8 %copy-start.21 = (bf16[64,4096]{1,0:T(8,128)(2,1)S(1)}, bf16[64,4096]{1,0:T(8,128)(2,1)}, u32[]{:S(2)}) copy-start(bf16[64,4096]{1,0:T(8,128)(2,1)} %copy-done.20) | copy-start | bytes 1572868
  759.3 14.1 %copy-start.92 = (f32[64]{0:T(128)S(1)}, f32[64]{0:T(128)}, u32[]{:S(2)}) copy-start(f32[64]{0:T(128)} %copy-done.91) | copy-start | bytes 772
  759.3 14.6 %copy-start.69 = (f32[64]{0:T(128)S(1)}, f32[64]{0:T(128)}, u32[]{:S(2)}) copy-start(f32[64]{0:T(128)} %copy-done.68) | copy-start | bytes 772
  759.3 13.8 %collective-permute-start.14 = (bf16[64,4096]{1,0:T(8,128)(2,1)}, bf16[64,4096]{1,0:T(8,128)(2,1)S(1)}, u32[]{:S(2)}, u32[]{:S(2)}) collective-permute-start(bf16[64,4096]{1,0:T(8,128)(2,1)} %get-tuple-element.126), channel_id=1, source_target_pairs={{0,64},{64,128},{128,192},{1,65},{65,129},{129,193},{2,66},{66,130... | collective-permute-start | bytes 1572872 | tf_op jit(solution)/shard_map/ppermute | solution.py:16
  778.0 12.9 %copy-start.28 = (bf16[64,4096]{1,0:T(8,128)(2,1)S(1)}, bf16[64,4096]{1,0:T(8,128)(2,1)}, u32[]{:S(2)}) copy-start(bf16[64,4096]{1,0:T(8,128)(2,1)} %copy-done.27) | copy-start | bytes 1572868
  778.0 13.2 %copy-start.94 = (f32[64]{0:T(128)S(1)}, f32[64]{0:T(128)}, u32[]{:S(2)}) copy-start(f32[64]{0:T(128)} %copy-done.93) | copy-start | bytes 772
  778.0 13.7 %copy-start.63 = (f32[64]{0:T(128)S(1)}, f32[64]{0:T(128)}, u32[]{:S(2)}) copy-start(f32[64]{0:T(128)} %copy-done.62) | copy-start | bytes 772
  778.0 12.9 %collective-permute-start.15 = (bf16[64,4096]{1,0:T(8,128)(2,1)}, bf16[64,4096]{1,0:T(8,128)(2,1)S(1)}, u32[]{:S(2)}, u32[]{:S(2)}) collective-permute-start(bf16[64,4096]{1,0:T(8,128)(2,1)} %get-tuple-element.128), channel_id=1, source_target_pairs={{0,64},{64,128},{128,192},{1,65},{65,129},{129,193},{2,66},{66,130... | collective-permute-start | bytes 1572872 | tf_op jit(solution)/shard_map/ppermute | solution.py:16
  798.1 12.6 %collective-permute-start.16 = (bf16[64,4096]{1,0:T(8,128)(2,1)S(1)}, bf16[64,4096]{1,0:T(8,128)(2,1)S(1)}, u32[]{:S(2)}, u32[]{:S(2)}) collective-permute-start(bf16[64,4096]{1,0:T(8,128)(2,1)S(1)} %fusion.115), channel_id=1, source_target_pairs={{64,0},{128,64},{192,128},{65,1},{129,65},{193,129},{66,2},{130,66... | collective-permute-start | bytes 1572872 | tf_op jit(solution)/shard_map/ppermute | solution.py:16
  799.6 11.3 copy-start.59
  812.3 11.1 copy-start.57
  812.3 10.9 collective-permute-start.17
  824.8 9.9 collective-permute-start.18
  836.3 10.1 collective-permute-start.19
  850.3 144.6 %copy-start.95 = (f32[8]{0:T(128)S(1)}, f32[8]{0:T(128)}, u32[]{:S(2)}) copy-start(f32[8]{0:T(128)} %psum.42) | copy-start | bytes 100
  (58 other events, 267.9 us)
Sparse Core Ops, SparseCore 0:
  11.4 81.5 all-gather.2
  260.3 141.7 reduce-scatter.2
  640.5 74.1 all-gather.4
  850.4 143.4 reduce-scatter.4
where the time goes:
time: 1240 us; the launch traced here: 1230 us
  waiting for transfers between devices  569 us (46%)
  blocking collectives  453 us (37%)
  matrix products  86.5 us (7%)
  starting transfers between devices  57.4 us (5%)
  other arithmetic  30.5 us (2%)
  local copies, waits for them, and re-layouts  19.7 us (2%)
  between operations  17.1 us (1%)
    reduce_scatter x2, waiting for transfers between devices, curvature_product(): lax.psum_scatter(term_sum, 'replica', scatter_dimension=2, tiled=True)  284 us
    psum x2, blocking collectives, per_device(): lax.psum(local_correlations(slot_bank, image), ('section', 'replica'))  159 us
    all_gather x2, waiting for transfers between devices, curvature_product(): tangent_full = lax.all_gather(tangent_shard, 'replica', axis=2, tiled=True)  148 us
    psum x2, blocking collectives, per_device(): lax.psum(jnp.sum(twice_clean * twice_clean), ('section', 'replica'))  147 us
    psum x2, blocking collectives, per_device(): lax.psum(local_correlations(slot_bank, cleaned), ('section', 'replica'))  147 us
    ppermute x20, waiting for transfers between devices, shifted(): return lax.ppermute(block, axis, route)  137 us
    dot_general x32, matrix products, against_rows(): lax.dot_general(left, right, (((1,), (1,)), ((), ())), preferred_element_...  64.6 us
    ppermute x20, starting transfers between devices, shifted(): return lax.ppermute(block, axis, route)  57.2 us
  transfers between devices with their start and end apart: 24, of which 20 were waited for; matrix products, arithmetic and copies ran while one was open for 4% of the time, Pallas kernels for 0%

commit v1 on v0

v1 whole, which is shorter than its diff:
```python
import functools

import jax
import jax.numpy as jnp
from jax import lax
from jax.experimental import pallas as pl
from jax.experimental.pallas import tpu as pltpu
from jax.sharding import PartitionSpec as P

ITERS = 2
NORM_EPS = 1e-05
VEC_EPS = 1e-06

YS, ZS, CS = 4, 8, 2
HALF = ZS // 2
TILE = 512
MESH = pl.DeviceIdType.MESH
F32 = jnp.float32
BF16 = jnp.bfloat16
VMEM_BYTES = 56 * 1024 * 1024
Y_CHUNKS = 2


def dot(left, right):
    return jnp.dot(left, right, preferred_element_type=F32)


def dot_t(left, right):
    return lax.dot_general(left, right, (((1,), (1,)), ((), ())), preferred_element_type=F32)


def over_tokens(left, right):
    return lax.dot_general(left, right, (((0,), (0,)), ((), ())), preferred_element_type=F32)


def two_parts(wide):
    high = wide.astype(BF16)
    return high, (wide - high.astype(F32)).astype(BF16)


class Refs:
    def __init__(self, names, refs):
        self.__dict__.update(zip(names, refs, strict=True))


class Place:
    def __init__(self, layers):
        self.layers = layers
        self.sec, rep = lax.axis_index("section"), lax.axis_index("replica")
        self.core = lax.rem(rep, CS)
        self.zed = lax.rem(rep // CS, ZS)
        self.why = rep // (CS * ZS)
        self.inner, self.outer = ZS * CS, layers * YS
        self.here, self.there = self.zed * CS + self.core, self.sec * YS + self.why
        self.sibling = self.device(self.sec, self.why, self.zed, 1 - self.core)

    def device(self, sec, why, zed, core):
        return (sec, (why * ZS + zed) * CS + core)

    def y_at(self, step):
        return lax.rem(self.why + step + YS, YS)

    def z_at(self, step):
        return lax.rem(self.zed + step + ZS, ZS)

    def x(self, step):
        return self.device(lax.rem(self.sec + step, self.layers), self.why, self.zed, self.core)

    def y(self, step):
        return self.device(self.sec, self.y_at(step), self.zed, self.core)

    def z(self, step):
        return self.device(self.sec, self.why, self.z_at(step), self.core)

    def near(self, step):
        return (self.sec, self.why * self.inner + lax.rem(self.here + step, self.inner))

    def far(self, step):
        other = lax.rem(self.there + step, self.outer)
        return (other // YS, lax.rem(other, YS) * self.inner + self.here)

    def slot(self, layer):
        return lax.rem(layer - self.sec + self.layers, self.layers)


def greet(partners):
    barrier = pltpu.get_barrier_semaphore()
    for partner in partners:
        pl.semaphore_signal(barrier, inc=1, device_id=partner, device_id_type=MESH)
    pl.semaphore_wait(barrier, len(partners))


def remote(src, dst, send_sem, recv_sem, partner):
    return pltpu.make_async_remote_copy(
        src_ref=src,
        dst_ref=dst,
        send_sem=send_sem,
        recv_sem=recv_sem,
        device_id=partner,
        device_id_type=MESH,
    )


def exchange(sends, count, partner, source, landing, send, recv):
    copies = []
    for step in range(1, count):
        copy = remote(source(step), landing(step), send.at[step - 1], recv.at[step - 1], partner(step))
        copy.start()
        copies.append(copy)
    sends += copies
    return copies


def arrived(ref, send, recv, at, partner):
    remote(ref, ref, send.at[at], recv.at[at], partner).wait_recv()


def drain(sends):
    for copy in sends:
        copy.wait_send()
    sends.clear()


def merged(*threads):
    threads = list(threads)
    while threads:
        for thread in list(threads):
            try:
                next(thread)
            except StopIteration:
                threads.remove(thread)
                continue
            yield


def finish(thread):
    for _ in thread:
        pass


GATHER_KINDS = 12


def gather_sems(blocks):
    first = blocks // 2
    dma = pltpu.SemaphoreType.DMA
    ring = (2 * ZS, first)
    return [dma((YS - 1,)), dma((YS - 1,)), dma(ring), dma(ring), dma(ring), dma(ring),
            dma((2 * ZS,)), dma((2 * ZS,)), dma((YS,)), dma((YS,)), dma((YS,)), dma((YS,))]


def ring_steps():
    return [(step, way) for step in range(1, HALF + 1) for way in (1, -1) if way > 0 or step < HALF]


def gather_first(out, blocks, at, sems, sends):
    ysend, yrecv, zsend, zrecv, csend, crecv = sems
    mine = out.at[pl.ds(blocks[0], len(blocks)), at.why, at.zed, at.core]
    exchange(sends, YS, at.y, lambda step: mine, lambda step: mine, ysend, yrecv)

    def bundle(chunk, z, core):
        return out.at[blocks[chunk], :, z, core]

    def index(step, way):
        return 2 * step + (way > 0)

    def send(step, way, chunk):
        view = bundle(chunk, at.z_at(-way * (step - 1)), at.core)
        copy = remote(view, view, zsend.at[index(step, way), chunk], zrecv.at[index(step, way), chunk],
                      at.z(way))
        copy.start()
        sends.append(copy)

    def hand_on(step, way, chunk):
        view = bundle(chunk, at.z_at(-way * step), at.core)
        copy = remote(view, view, csend.at[index(step, way), chunk], crecv.at[index(step, way), chunk],
                      at.sibling)
        copy.start()
        sends.append(copy)

    yield
    for step in range(1, YS):
        block = out.at[pl.ds(blocks[0], len(blocks)), at.y_at(-step), at.zed, at.core]
        arrived(block, ysend, yrecv, step - 1, at.sibling)
    for chunk in range(len(blocks)):
        send(1, 1, chunk)
        send(1, -1, chunk)
    for chunk in range(len(blocks)):
        hand_on(0, 1, chunk)
    steps = ring_steps()
    for step in range(1, HALF + 1):
        for chunk in range(len(blocks)):
            yield
            for way in (1, -1):
                if (step, way) not in steps:
                    continue
                view = bundle(chunk, at.z_at(-way * step), at.core)
                remote(view, view, zsend.at[index(step, way), chunk], zrecv.at[index(step, way), chunk],
                       at.sibling).wait_recv()
                if (step + 1, way) in steps:
                    send(step + 1, way, chunk)
                hand_on(step, way, chunk)
    for step, way in [(0, 1)] + steps:
        yield
        for chunk in range(len(blocks)):
            view = bundle(chunk, at.z_at(-way * step), 1 - at.core)
            remote(view, view, csend.at[index(step, way), chunk], crecv.at[index(step, way), chunk],
                   at.sibling).wait_recv()


def gather_second(out, blocks, at, sems, sends):
    zsend, zrecv, ysend, yrecv, csend, crecv = sems
    span = pl.ds(blocks[0], len(blocks))

    def view(z):
        return out.at[span, at.why, z, at.core]

    def index(step, way):
        return 2 * step + (way > 0)

    def send(step, way):
        block = view(at.z_at(-way * (step - 1)))
        copy = remote(block, block, zsend.at[index(step, way)], zrecv.at[index(step, way)], at.z(way))
        copy.start()
        sends.append(copy)

    def bundle(step, core, part=None):
        zeds = pl.ds(0, ZS) if part is None else pl.ds(part * HALF, HALF)
        return out.at[span, at.y_at(step), zeds, core]

    def along(ref, idx, way):
        copy = remote(ref, ref, ysend.at[idx], yrecv.at[idx], at.y(way))
        copy.start()
        sends.append(copy)

    def hand_on(step, idx):
        ref = bundle(step, at.core)
        copy = remote(ref, ref, csend.at[idx], crecv.at[idx], at.sibling)
        copy.start()
        sends.append(copy)

    send(1, 1)
    send(1, -1)
    steps = ring_steps()
    for step in range(1, HALF + 1):
        yield
        for way in (1, -1):
            if (step, way) not in steps:
                continue
            block = view(at.z_at(-way * step))
            remote(block, block, zsend.at[index(step, way)], zrecv.at[index(step, way)],
                   at.sibling).wait_recv()
            if (step + 1, way) in steps:
                send(step + 1, way)
    along(bundle(0, at.core), 0, 1)
    along(bundle(0, at.core), 1, -1)
    hand_on(0, 0)
    yield
    arrived(bundle(-1, at.core), ysend, yrecv, 0, at.sibling)
    along(bundle(-1, at.core, 0), 2, 1)
    arrived(bundle(1, at.core), ysend, yrecv, 1, at.sibling)
    along(bundle(1, at.core, 1), 3, -1)
    hand_on(-1, 1)
    hand_on(1, 2)
    yield
    arrived(bundle(2, at.core, 0), ysend, yrecv, 2, at.sibling)
    arrived(bundle(2, at.core, 1), ysend, yrecv, 3, at.sibling)
    hand_on(2, 3)
    for idx, step in enumerate((0, -1, 1, 2)):
        yield
        arrived(bundle(step, 1 - at.core), csend, crecv, idx, at.sibling)


def gather(out, start, count, at, sems, sends):
    half = count // 2
    first = list(range(start, start + half))
    second = list(range(start + half, start + count))
    return merged(gather_second(out, second, at, sems[6:], sends),
                  gather_first(out, first, at, sems[:6], sends))


def row_block(ref, block, idx):
    per = TILE // (CS * 64)
    wide = ref[block, idx // (ZS // per), pl.ds((idx % (ZS // per)) * per, per)]
    return wide.reshape(TILE, 128)


def tiles(full_d, body):
    def step(idx, carry):
        body(idx, pl.ds(pl.multiple_of(idx * TILE, TILE), TILE))
        return carry
    lax.fori_loop(0, full_d // TILE, step, 0)


def lane_sums(wide):
    return sum(wide[:, start:start + 128] for start in range(0, TILE, 128))


def primal(ref, at, full_d, between):
    layers, sec = at.layers, at.sec
    tokens = ref.rows.shape[0]
    part = tokens // layers
    acc, along = ref.acc, ref.along
    mine = pl.ds(pl.multiple_of(sec * part, part), part)
    along[0] = jnp.zeros((tokens, 128), F32)

    def rows_of(layer, where, cols):
        return ref.rows[where, cols] if layer == 0 else ref.every_row[layer - 1, where, cols]

    everywhere = slice(None)

    def square(idx, cols):
        wide = ref.rows[:, cols].astype(F32)
        along[0] += lane_sums(wide * wide)
    tiles(full_d, square)
    for layer in range(layers):
        down, up = 2 * at.slot(layer), 2 * at.slot(layer) + 1
        mean = jnp.sum(along[0], axis=-1, keepdims=True) * (1.0 / full_d)
        inv = lax.rsqrt(mean + NORM_EPS)
        acc[0] = jnp.zeros((tokens, 128), F32)

        def project(idx, cols):
            gain = ref.gains[at.slot(layer), :, cols]
            piece = (rows_of(layer, everywhere, cols).astype(F32) * inv * gain).astype(BF16)

            @pl.when(sec == layer)
            def _():
                ref.normed[:, cols] = piece
            acc[0] += dot(piece, row_block(ref.weights, down, idx))
        tiles(full_d, project)
        between()
        pre = acc[0]
        sig = jax.nn.sigmoid(pre)
        act = (pre * sig).astype(BF16)
        ref.hidden[:, layer * 128:(layer + 1) * 128] = act

        @pl.when(sec == layer)
        def _():
            ref.own_hidden[...] = act
        ref.pre_act[layer] = pre
        ref.slope[layer] = sig + pre * sig * (1.0 - sig)
        ref.inv_rms[layer] = jnp.broadcast_to(inv, (tokens, 128))
        along[0] = jnp.zeros((tokens, 128), F32)
        if layer + 1 < layers:
            def forward(idx, cols):
                wide = rows_of(layer, everywhere, cols).astype(F32)
                wide = wide + dot_t(act, row_block(ref.weights, up, idx))
                rounded = wide.astype(BF16)
                ref.every_row[layer, :, cols] = rounded
                again = rounded.astype(F32)
                along[0] += lane_sums(again * again)
            tiles(full_d, forward)
            between()
    ref.uu[...] = jnp.zeros_like(ref.uu)
    ref.ud[...] = jnp.zeros_like(ref.ud)
    ref.row_up[...] = jnp.zeros_like(ref.row_up)

    def grams(idx, cols):
        ups = [row_block(ref.weights, 2 * at.slot(layer) + 1, idx) for layer in range(layers)]
        every = jnp.concatenate(ups, axis=1)
        turned = every.T
        ref.uu[...] += dot(turned, every)
        pair_at = 0
        for layer in range(1, layers):
            width = layer * 128
            gain = ref.gains[at.slot(layer), :, cols]
            high, low = two_parts(turned[:width].astype(F32) * gain)
            down = row_block(ref.weights, 2 * at.slot(layer), idx)
            pair = dot(high, down) + dot(low, down)
            block = dot(rows_of(layer, mine, cols), every[:, :width])
            for k in range(layer):
                ref.ud[pair_at] += pair[k * 128:(k + 1) * 128]
                ref.row_up[pair_at] += block[:, k * 128:(k + 1) * 128]
                pair_at += 1
    tiles(full_d, grams)
    between()
    ref.uu_high[...], ref.uu_low[...] = two_parts(ref.uu[...])
    ref.ud_high[...], ref.ud_low[...] = two_parts(ref.ud[...])
    ref.gram[...] = over_tokens(ref.hidden[...], ref.own_hidden[...])


def recurrence(tan_base, back_base, pre_act, slope, inv_rms, row_up, up_up, up_down, full_d):
    layers = len(tan_base)
    tan_act = []
    for layer in range(layers):
        tan_pre = tan_base[layer]
        if layer > 0:
            moved = sum(dot(tan_act[k], up_down[k][layer][0]) + dot(tan_act[k], up_down[k][layer][1])
                        for k in range(layer))
            along = sum(jnp.sum(tan_act[k].astype(F32) * row_up[layer][k], axis=-1, keepdims=True)
                        for k in range(layer))
            inv = inv_rms[layer]
            tan_pre = tan_pre + inv * moved - (inv * inv * (1.0 / full_d)) * along * pre_act[layer]
        tan_act.append((tan_pre * slope[layer]).astype(BF16))
    every = jnp.concatenate(tan_act, axis=1)
    back_all = dot(every, up_up[0]) + dot(every, up_up[1])
    back_pre, moved_back, pull = {}, {}, {}
    for layer in reversed(range(layers)):
        back_act = back_base[layer] + back_all[:, layer * 128:(layer + 1) * 128]
        for k in range(layer + 1, layers):
            back_act = back_act + dot_t(moved_back[k], up_down[layer][k][0])
            back_act = back_act + dot_t(moved_back[k], up_down[layer][k][1])
            back_act = back_act - pull[k] * row_up[k][layer]
        piece = (back_act * slope[layer]).astype(BF16)
        wide = piece.astype(F32)
        inv = inv_rms[layer]
        back_pre[layer] = piece
        moved_back[layer] = (wide * inv).astype(BF16)
        pull[layer] = inv * inv * (1.0 / full_d) * jnp.sum(wide * pre_act[layer], axis=-1, keepdims=True)
    return tan_act + [back_pre[layer] for layer in range(layers)]


def token_terms(ref, at, full_d):
    layers, sec = at.layers, at.sec
    acc, along = ref.acc, ref.along
    acc[...] = jnp.zeros_like(acc)
    along[...] = jnp.zeros_like(along)
    own_hidden = ref.own_hidden[...]
    part = own_hidden.shape[0] // layers

    def body(idx, cols):
        acc[0] += dot(ref.normed[:, cols], row_block(ref.vector, 0, idx))
        spread = dot_t(own_hidden, row_block(ref.vector, 1, idx))
        rounded = spread.astype(BF16)
        for layer in range(layers):
            acc[layers + layer] += dot(rounded, row_block(ref.weights, 2 * at.slot(layer) + 1, idx))
        for layer in range(1, layers):
            scaled = (spread * ref.gains[at.slot(layer), :, cols]).astype(BF16)
            acc[layer] += dot(scaled, row_block(ref.weights, 2 * at.slot(layer), idx))
            along[layer] += lane_sums(ref.every_row[layer - 1, :, cols].astype(F32) * spread)
    tiles(full_d, body)
    base = acc[0]

    def put(block, value):
        value = value.astype(BF16)
        for quarter in range(layers):
            ref.pay[quarter, :, block * 128:(block + 1) * 128] = value[quarter * part:(quarter + 1) * part]
    for layer in range(layers):
        own = jnp.where(sec == layer, base, 0.0)
        if layer > 0:
            inv = ref.inv_rms[layer]
            reach = jnp.sum(along[layer], axis=-1, keepdims=True)
            later = inv * acc[layer] - (inv * inv * (1.0 / full_d)) * reach * ref.pre_act[layer]
            own = own + jnp.where(sec < layer, later, 0.0)
        put(layer, own)
        put(layers + layer, acc[layers + layer])


def gradient_terms(ref, at, full_d):
    layers, sec = at.layers, at.sec
    res = ref.result
    part = res.shape[1]
    tokens = part * layers

    def column(block):
        return jnp.concatenate([res[q, :, block * 128:(block + 1) * 128] for q in range(layers)], axis=0)
    back = [column(layers + layer) for layer in range(layers)]
    pulls, moved = [], []
    for layer in range(layers):
        inv = ref.inv_rms[layer]
        wide = back[layer].astype(F32)
        pull = inv * inv * (1.0 / full_d) * jnp.sum(wide * ref.pre_act[layer], axis=-1, keepdims=True)
        pulls.append(jnp.where(sec < layer, pull, 0.0))
        moved.append(jnp.where(sec < layer, wide * inv, 0.0).astype(BF16))
    acts = []
    later = jnp.zeros((tokens, 128), F32)
    for layer in reversed(range(layers)):
        old = ref.hidden[:, layer * 128:(layer + 1) * 128].astype(F32)
        acts.insert(0, (column(layer).astype(F32) - later * old).astype(BF16))
        later = later + pulls[layer]
    total = later[:, :1]
    own_back = back[0]
    for layer in range(1, layers):
        own_back = jnp.where(sec == layer, back[layer], own_back)
    own_hidden = ref.own_hidden[...]
    per = TILE // (CS * 64)

    def body(idx, cols):
        cot = -total * ref.rows[:, cols].astype(F32)
        for layer in range(layers):
            cot = cot + dot_t(acts[layer], row_block(ref.weights, 2 * at.slot(layer) + 1, idx))
        for layer in range(1, layers):
            cot = cot + (dot_t(moved[layer], row_block(ref.weights, 2 * at.slot(layer), idx))
                         * ref.gains[at.slot(layer), :, cols])
        where = (idx // (ZS // per), pl.ds((idx % (ZS // per)) * per, per))
        ref.part_b[where] = over_tokens(cot.astype(BF16), own_hidden).reshape(per, CS, 64, 128)
        ref.part_a[where] = over_tokens(ref.normed[:, cols], own_back).reshape(per, CS, 64, 128)
        for copy in swap_copies(ref, at, idx):
            copy.start()
    tiles(full_d, body)


def swap_copies(ref, at, idx):
    per = TILE // (CS * 64)
    where = (idx // (ZS // per), pl.ds((idx % (ZS // per)) * per, per))
    other = where + (1 - at.core,)
    return (
        remote(ref.part_b.at[other], ref.swap_b.at[where], ref.swap_send.at[0, idx], ref.swap_recv.at[0, idx],
               at.sibling),
        remote(ref.part_a.at[other], ref.swap_a.at[where], ref.swap_send.at[1, idx], ref.swap_recv.at[1, idx],
               at.sibling),
    )


def scatter_first(ref, at, sends, done):
    left_in, right_in, y_in = ref.left_in, ref.right_in, ref.y_a
    size = YS // Y_CHUNKS

    def chunk_of(chunk):
        return pl.ds(chunk * size, size)

    def chip_sum(z, chunk):
        span = chunk_of(chunk)
        return ref.swap_a[span, z] + ref.part_a[span, z, at.core]

    def left(step, chunk):
        z = at.z_at(step - HALF - 1)
        return remote(ref.out_a.at[chunk_of(chunk), z], left_in.at[step - 1, chunk_of(chunk)],
                      ref.ls.at[step - 1, chunk], ref.lr.at[step - 1, chunk], at.z(-1))

    def right(step, chunk):
        z = at.z_at(HALF - step)
        return remote(ref.out_a.at[chunk_of(chunk), z], right_in.at[step - 1, chunk_of(chunk)],
                      ref.rs.at[step - 1, chunk], ref.rr.at[step - 1, chunk], at.z(1))

    def go(copy):
        copy.start()
        sends.append(copy)

    for step in range(1, HALF + 1):
        for chunk in range(Y_CHUNKS):
            if step > 1:
                yield
            span = chunk_of(chunk)
            z = at.z_at(step - HALF - 1)
            value = chip_sum(z, chunk)
            if step > 1:
                left(step - 1, chunk).wait_recv()
                value = value + left_in[step - 2, span]
            ref.out_a[span, z] = value
            go(left(step, chunk))
            if step < HALF:
                z = at.z_at(HALF - step)
                value = chip_sum(z, chunk)
                if step > 1:
                    right(step - 1, chunk).wait_recv()
                    value = value + right_in[step - 2, span]
                ref.out_a[span, z] = value
                go(right(step, chunk))
    yield
    for chunk in range(Y_CHUNKS):
        span = chunk_of(chunk)
        value = chip_sum(at.zed, chunk)
        right(HALF - 1, chunk).wait_recv()
        value = value + right_in[HALF - 2, span]
        left(HALF, chunk).wait_recv()
        ref.out_a[span, at.zed] = value + left_in[HALF - 1, span]

    copies = exchange(sends, YS, at.y, lambda step: ref.out_a.at[at.y_at(step), at.zed],
                      lambda step: y_in.at[step - 1], ref.yas, ref.yar)
    yield
    value = ref.out_a[at.why, at.zed]
    for step, copy in enumerate(copies):
        copy.wait_recv()
        value = value + y_in[step]
    done.append(value)


def scatter_second(ref, at, sends, done):
    halves = (pl.ds(0, HALF), pl.ds(HALF, HALF))
    out = ref.out_b

    def chip_sum(step, half):
        y = at.y_at(step)
        return ref.swap_b[y, halves[half]] + ref.part_b[y, halves[half], at.core]

    def go(src, dst, idx, way):
        copy = remote(src, dst, ref.ybs.at[idx], ref.ybr.at[idx], at.y(way))
        copy.start()
        sends.append(copy)

    def took(dst, idx):
        arrived(dst, ref.ybs, ref.ybr, idx, at.sibling)

    def view(step, half):
        return out.at[at.y_at(step), halves[half]]

    out[at.y_at(2), halves[0]] = chip_sum(2, 0)
    go(view(2, 0), ref.chain.at[0], 0, 1)
    out[at.y_at(2), halves[1]] = chip_sum(2, 1)
    go(view(2, 1), ref.chain.at[1], 1, -1)
    out[at.y_at(1), halves[1]] = chip_sum(1, 1)
    go(view(1, 1), ref.from_low.at[halves[1]], 2, 1)
    out[at.y_at(-1), halves[0]] = chip_sum(-1, 0)
    go(view(-1, 0), ref.from_high.at[halves[0]], 3, -1)
    yield
    took(ref.chain.at[0], 0)
    out[at.y_at(1), halves[0]] = chip_sum(1, 0) + ref.chain[0]
    go(view(1, 0), ref.from_low.at[halves[0]], 4, 1)
    took(ref.chain.at[1], 1)
    out[at.y_at(-1), halves[1]] = chip_sum(-1, 1) + ref.chain[1]
    go(view(-1, 1), ref.from_high.at[halves[1]], 5, -1)
    yield
    yield
    yield
    took(ref.from_low.at[halves[1]], 2)
    took(ref.from_high.at[halves[0]], 3)
    took(ref.from_low.at[halves[0]], 4)
    took(ref.from_high.at[halves[1]], 5)
    for half in range(2):
        out[at.why, halves[half]] = (
            chip_sum(0, half) + ref.from_low[halves[half]] + ref.from_high[halves[half]])
    copies = exchange(sends, ZS, at.z, lambda step: out.at[at.why, at.z_at(step)],
                      lambda step: ref.z_b.at[step - 1], ref.zbs, ref.zbr)
    yield
    yield
    yield
    value = out[at.why, at.zed]
    for step, copy in enumerate(copies):
        copy.wait_recv()
        value = value + ref.z_b[step]
    done.append(value)


def scatter_sum(ref, at, full_d, sends):
    for idx in range(full_d // TILE):
        for copy in swap_copies(ref, at, idx):
            copy.wait_recv()
            sends.append(copy)
    done_a, done_b = [], []
    finish(merged(scatter_second(ref, at, sends, done_b), scatter_first(ref, at, sends, done_a)))
    return done_a[0], done_b[0]


def gram_steps(ref, at, sends):
    gram, whole = ref.gram, ref.hidden_gram
    piece = gram.shape[0] // at.inner
    small = piece // YS

    def rows(index, size):
        return pl.ds(pl.multiple_of(index * size, size), size)

    copies = exchange(sends, at.inner, at.near,
                      lambda step: gram.at[rows(lax.rem(at.here + step, at.inner), piece)],
                      lambda step: ref.gram_in.at[step - 1], ref.g1s, ref.g1r)
    yield
    value = gram[rows(at.here, piece), :]
    for step, copy in enumerate(copies):
        copy.wait_recv()
        value = value + ref.gram_in[step]
    ref.gram_sum[...] = value
    copies = exchange(sends, YS, at.y, lambda step: ref.gram_sum.at[rows(at.y_at(step), small)],
                      lambda step: ref.gram_in2.at[step - 1], ref.g2s, ref.g2r)
    yield
    own = rows(at.why, small)
    value = ref.gram_sum[own, :]
    for step, copy in enumerate(copies):
        copy.wait_recv()
        value = value + ref.gram_in2[step]
    ref.gram_out[own, :] = value
    exchange(sends, YS, at.y, lambda step: ref.gram_out.at[own], lambda step: ref.gram_out.at[own],
             ref.g3s, ref.g3r)
    yield
    for step in range(1, YS):
        arrived(ref.gram_out.at[rows(at.y_at(-step), small)], ref.g3s, ref.g3r, step - 1, at.sibling)
    mine = rows(at.here, piece)
    whole[mine, :] = ref.gram_out[...]
    exchange(sends, at.inner, at.near, lambda step: ref.gram_out, lambda step: whole.at[mine],
             ref.g4s, ref.g4r)
    yield
    for step in range(1, at.inner):
        source = rows(lax.rem(at.here + at.inner - step, at.inner), piece)
        arrived(whole.at[source], ref.g4s, ref.g4r, step - 1, at.sibling)


def sum_all(ref, at, line, sends):
    vec, near, far, half_sum = ref.vec, ref.near, ref.far, ref.half_sum
    vec[...] = jnp.broadcast_to(line, vec.shape)
    exchange(sends, at.inner, at.near, lambda step: vec, lambda step: near.at[at.here], ref.ns, ref.nr)
    near[at.here] = vec[...]
    for step in range(1, at.inner):
        slot = near.at[lax.rem(at.here + at.inner - step, at.inner)]
        arrived(slot, ref.ns, ref.nr, step - 1, at.sibling)
    half_sum[...] = jnp.sum(near[...], axis=0)
    exchange(sends, at.outer, at.far, lambda step: half_sum, lambda step: far.at[at.there], ref.fs, ref.fr)
    far[at.there] = half_sum[...]
    for step in range(1, at.outer):
        slot = far.at[lax.rem(at.there + at.outer - step, at.outer)]
        arrived(slot, ref.fs, ref.fr, step - 1, at.sibling)
    return jnp.sum(far[...], axis=0)[:1]


def put_vector(ref, at, down_rows, up_rows, full_d, rank, sends):
    ref.shard[0] = (down_rows * (full_d ** -0.5)).astype(BF16)
    ref.shard[1] = (up_rows * (rank ** -0.5)).astype(BF16)
    ref.vector[:, at.why, at.zed, at.core] = ref.shard[...]
    ref.ups[0] = ref.shard[1]
    exchange(sends, at.layers, at.x, lambda step: ref.shard.at[1],
             lambda step: ref.ups.at[at.layers - step], ref.x3s, ref.x3r)


def ups_arrived(ref, at):
    for step in range(1, at.layers):
        arrived(ref.ups.at[at.layers - step], ref.x3s, ref.x3r, step - 1, at.sibling)


def curvature(ref, at, full_d, sends, between):
    layers, sec = at.layers, at.sec
    token_terms(ref, at, full_d)
    pay = ref.pay
    copies = exchange(sends, layers, at.x, lambda step: pay.at[lax.rem(sec + step, layers)],
                      lambda step: ref.pay_in.at[step - 1], ref.x1s, ref.x1r)
    total = pay[sec].astype(F32)
    for step, copy in enumerate(copies):
        copy.wait_recv()
        total = total + ref.pay_in[step].astype(F32)
    between()
    row_up = {}
    up_down = {k: {} for k in range(layers)}
    idx = 0
    for layer in range(layers):
        for k in range(layer):
            row_up.setdefault(layer, {})[k] = ref.row_up[idx]
            up_down[k][layer] = (ref.ud_high[idx], ref.ud_low[idx])
            idx += 1
    part = pay.shape[1]
    mine = pl.ds(pl.multiple_of(sec * part, part), part)
    pieces = recurrence(
        [total[:, start * 128:(start + 1) * 128] for start in range(layers)],
        [total[:, start * 128:(start + 1) * 128] for start in range(layers, 2 * layers)],
        [ref.pre_act[layer, mine, :] for layer in range(layers)],
        [ref.slope[layer, mine, :] for layer in range(layers)],
        [ref.inv_rms[layer, mine, :] for layer in range(layers)],
        row_up, (ref.uu_high[...], ref.uu_low[...]), up_down, full_d)
    result = ref.result
    result[sec] = jnp.concatenate(pieces, axis=1)
    own = result.at[sec]
    exchange(sends, layers, at.x, lambda step: own, lambda step: own, ref.x2s, ref.x2r)
    between()
    for step in range(1, layers):
        arrived(result.at[lax.rem(sec + layers - step, layers)], ref.x2s, ref.x2r, step - 1, at.sibling)
    between()
    gradient_terms(ref, at, full_d)
    return scatter_sum(ref, at, full_d, sends)


def main_kernel(cfg, names, *refs):
    layers, tokens_all, base_count = cfg
    ref = Refs(names, refs)
    at = Place(layers)
    full_d, rank = ref.rows.shape[1], ref.down.shape[-1]
    sends = []
    lane = lax.broadcasted_iota(jnp.int32, (1, 128), 1)
    copies = [pltpu.make_async_copy(ref.down, ref.weights.at[0], ref.local.at[0]),
              pltpu.make_async_copy(ref.up, ref.weights.at[1], ref.local.at[1])]
    for copy in copies:
        copy.start()
    ref.gains[0] = ref.gain[...]
    greet([at.near(step) for step in range(1, at.inner)] + [at.far(step) for step in range(1, at.outer)])

    for block, source in enumerate((ref.down, ref.up)):
        row = source.at[at.why, at.zed, at.core]
        exchange(sends, layers, at.x, lambda step: row,
                 lambda step: ref.weights.at[2 * (layers - step) + block, at.why, at.zed, at.core],
                 ref.xws.at[block], ref.xwr.at[block])
    exchange(sends, layers, at.x, lambda step: ref.gain, lambda step: ref.gains.at[layers - step],
             ref.xgs, ref.xgr)
    put_vector(ref, at, ref.basis[base_count - 1, 0], ref.basis[base_count - 1, 1], full_d, rank, sends)
    for step in range(1, layers):
        for block in range(2):
            arrived(ref.weights.at[2 * (layers - step) + block, at.why, at.zed, at.core],
                    ref.xws.at[block], ref.xwr.at[block], step - 1, at.sibling)
    sems = [ref.__dict__[key] for key in range(2 * GATHER_KINDS)]
    finish(gather(ref.weights, 2, 2 * layers - 2, at, sems[:GATHER_KINDS], sends))
    for step in range(1, layers):
        arrived(ref.gains.at[layers - step], ref.xgs, ref.xgr, step - 1, at.sibling)
    for copy in copies:
        copy.wait()
    moving = gather(ref.vector, 0, 2, at, sems[GATHER_KINDS:], sends)

    def move():
        next(moving, None)
        next(moving, None)
    move()
    primal(ref, at, full_d, move)
    finish(moving)
    ups_arrived(ref, at)
    drain(sends)

    norm = 1.0 / tokens_all
    scales = (full_d ** -0.5, rank ** -0.5)
    held = [(ref.basis[k, 0], ref.basis[k, 1]) for k in range(base_count)]
    gram_slots = {}

    def gram_at(k, j):
        return gram_slots[max(k, j), min(k, j)]

    def inner_sum(left, right):
        both = left[0] * right[0] + left[1] * right[1]
        return jnp.sum(jnp.sum(both, axis=0, keepdims=True), axis=1, keepdims=True)

    for it in range(ITERS):
        count = base_count + it
        summing = gram_steps(ref, at, sends) if it == 0 else iter(())
        next(summing, None)
        sum_a, sum_b = curvature(ref, at, full_d, sends, lambda: next(summing, None))
        finish(summing)
        for layer in range(layers):
            wide = ref.hidden_gram[layer * rank:(layer + 1) * rank, :]
            high = wide.astype(BF16)
            rest = wide - high.astype(F32)
            middle, low = two_parts(rest)
            ups = ref.ups[at.slot(layer)]
            sum_b = sum_b + dot(ups, high) + dot(ups, middle) + dot(ups, low)
        image = [sum_a * (scales[0] * norm), sum_b * (scales[1] * norm)]

        pairs = [(k, j) for k in range(count) for j in range(k + 1) if (k, j) not in gram_slots]
        values = [inner_sum(item, image) for item in held] + [inner_sum(image, image)]
        values += [inner_sum(held[k], held[j]) for k, j in pairs]
        line = jnp.zeros((1, 128), F32)
        for place, value in enumerate(values):
            line = jnp.where(lane == place, value, line)
        line = sum_all(ref, at, line, sends) * (1.0 / (layers * 2 * full_d * rank))
        totals = [jnp.sum(jnp.where(lane == place, line, 0.0), axis=1, keepdims=True)
                  for place in range(len(values))]
        first_coef, image_square = totals[:count], totals[count]
        gram_slots.update(zip(pairs, totals[count + 1:]))
        coef, length_square = [], image_square
        for k in range(count):
            again = sum(gram_at(k, j) * first_coef[j] for j in range(count))
            coef.append(first_coef[k] + (first_coef[k] - again))
        for k in range(count):
            mixed = sum(gram_at(k, j) * coef[j] for j in range(count))
            length_square = length_square + coef[k] * (mixed - 2.0 * first_coef[k])
        length = jnp.sqrt(jnp.maximum(length_square, 0.0) + VEC_EPS)
        fresh = []
        for block in range(2):
            clean = image[block]
            for k in range(count):
                clean = clean - coef[k] * held[k][block]
            fresh.append(clean / length)
            ref.fresh[it, block] = fresh[block]
        line = jnp.zeros((1, 128), F32)
        for k in range(count):
            line = jnp.where(lane == k, coef[k], line)
        line = jnp.where(lane == base_count + ITERS, length, line)
        ref.hess[it] = jnp.broadcast_to(line, (8, 128))
        drain(sends)
        if it + 1 < ITERS:
            held.append((ref.fresh[it, 0], ref.fresh[it, 1]))
            put_vector(ref, at, fresh[0], fresh[1], full_d, rank, sends)
            finish(gather(ref.vector, 0, 2, at, sems[GATHER_KINDS:], sends))
            ups_arrived(ref, at)
            drain(sends)


def per_device(hidden_in, down_weight, up_weight, norm_gain, krylov_basis):
    layers = lax.axis_size("section")
    micro, tok, full_d = hidden_in.shape
    rank = down_weight.shape[2]
    tokens = micro * tok
    part = tokens // layers
    basis = krylov_basis[:, 0]
    base_count, _, rows, _ = basis.shape
    split = (YS, ZS, CS, rows, rank)
    vmem = pl.BlockSpec(memory_space=pltpu.VMEM)
    hbm = pl.BlockSpec(memory_space=pl.ANY)
    dma = pltpu.SemaphoreType.DMA
    inner, outer = ZS * CS, layers * YS
    pairs = layers * (layers - 1) // 2
    wide = layers * rank
    piece = wide // inner

    inputs = dict(
        rows=hidden_in.reshape(tokens, full_d),
        down=down_weight[0].reshape(split),
        up=up_weight[0].reshape(split),
        gain=norm_gain,
        basis=basis,
    )
    outputs = dict(
        fresh=jax.ShapeDtypeStruct((ITERS, 2, rows, rank), F32),
        hess=jax.ShapeDtypeStruct((ITERS, 8, 128), F32),
    )
    scratch = dict(
        weights=pltpu.VMEM((2 * layers,) + split, BF16),
        vector=pltpu.VMEM((2,) + split, BF16),
        gains=pltpu.VMEM((layers, 1, full_d), F32),
        ups=pltpu.VMEM((layers, rows, rank), BF16),
        shard=pltpu.VMEM((2, rows, rank), BF16),
        every_row=pltpu.VMEM((layers - 1, tokens, full_d), BF16),
        normed=pltpu.VMEM((tokens, full_d), BF16),
        hidden=pltpu.VMEM((tokens, wide), BF16),
        own_hidden=pltpu.VMEM((tokens, rank), BF16),
        pre_act=pltpu.VMEM((layers, tokens, rank), F32),
        slope=pltpu.VMEM((layers, tokens, rank), F32),
        inv_rms=pltpu.VMEM((layers, tokens, 128), F32),
        row_up=pltpu.VMEM((pairs, part, rank), F32),
        uu=pltpu.VMEM((wide, wide), F32),
        ud=pltpu.VMEM((pairs, rank, rank), F32),
        uu_high=pltpu.VMEM((wide, wide), BF16),
        uu_low=pltpu.VMEM((wide, wide), BF16),
        ud_high=pltpu.VMEM((pairs, rank, rank), BF16),
        ud_low=pltpu.VMEM((pairs, rank, rank), BF16),
        gram=pltpu.VMEM((wide, rank), F32),
        hidden_gram=pltpu.VMEM((wide, rank), F32),
        gram_in=pltpu.VMEM((inner - 1, piece, rank), F32),
        gram_sum=pltpu.VMEM((piece, rank), F32),
        gram_in2=pltpu.VMEM((YS - 1, piece // YS, rank), F32),
        gram_out=pltpu.VMEM((piece, rank), F32),
        acc=pltpu.VMEM((2 * layers, tokens, rank), F32),
        along=pltpu.VMEM((layers, tokens, 128), F32),
        pay=pltpu.VMEM((layers, part, 2 * wide), BF16),
        pay_in=pltpu.VMEM((layers - 1, part, 2 * wide), BF16),
        result=pltpu.VMEM((layers, part, 2 * wide), BF16),
        part_a=pltpu.VMEM(split, F32),
        part_b=pltpu.VMEM(split, F32),
        swap_a=pltpu.VMEM((YS, ZS, rows, rank), F32),
        swap_b=pltpu.VMEM((YS, ZS, rows, rank), F32),
        out_a=pltpu.VMEM((YS, ZS, rows, rank), F32),
        out_b=pltpu.VMEM((YS, ZS, rows, rank), F32),
        left_in=pltpu.VMEM((HALF, YS, rows, rank), F32),
        right_in=pltpu.VMEM((HALF - 1, YS, rows, rank), F32),
        y_a=pltpu.VMEM((YS - 1, rows, rank), F32),
        chain=pltpu.VMEM((2, HALF, rows, rank), F32),
        from_low=pltpu.VMEM((ZS, rows, rank), F32),
        from_high=pltpu.VMEM((ZS, rows, rank), F32),
        z_b=pltpu.VMEM((ZS - 1, rows, rank), F32),
        vec=pltpu.VMEM((8, 128), F32),
        near=pltpu.VMEM((inner, 8, 128), F32),
        far=pltpu.VMEM((outer, 8, 128), F32),
        half_sum=pltpu.VMEM((8, 128), F32),
        local=dma((2,)),
        xws=dma((2, layers - 1)), xwr=dma((2, layers - 1)),
        xgs=dma((layers - 1,)), xgr=dma((layers - 1,)),
        x1s=dma((layers - 1,)), x1r=dma((layers - 1,)),
        x2s=dma((layers - 1,)), x2r=dma((layers - 1,)),
        x3s=dma((layers - 1,)), x3r=dma((layers - 1,)),
        g1s=dma((inner - 1,)), g1r=dma((inner - 1,)),
        g2s=dma((YS - 1,)), g2r=dma((YS - 1,)),
        g3s=dma((YS - 1,)), g3r=dma((YS - 1,)),
        g4s=dma((inner - 1,)), g4r=dma((inner - 1,)),
        swap_send=dma((2, full_d // TILE)), swap_recv=dma((2, full_d // TILE)),
        ls=dma((HALF, Y_CHUNKS)), lr=dma((HALF, Y_CHUNKS)),
        rs=dma((HALF - 1, Y_CHUNKS)), rr=dma((HALF - 1, Y_CHUNKS)),
        yas=dma((YS - 1,)), yar=dma((YS - 1,)),
        ybs=dma((6,)), ybr=dma((6,)),
        zbs=dma((ZS - 1,)), zbr=dma((ZS - 1,)),
        ns=dma((inner - 1,)), nr=dma((inner - 1,)),
        fs=dma((outer - 1,)), fr=dma((outer - 1,)),
    )
    scratch.update(enumerate(gather_sems(2 * layers - 2) + gather_sems(2)))
    names = list(inputs) + list(outputs) + list(scratch)
    cfg = (layers, tokens * lax.axis_size("replica"), base_count)
    fresh, hess = pl.pallas_call(
        functools.partial(main_kernel, cfg, names),
        out_shape=tuple(outputs.values()),
        in_specs=[vmem, hbm, hbm, vmem, vmem],
        out_specs=(vmem, vmem),
        scratch_shapes=list(scratch.values()),
        compiler_params=pltpu.CompilerParams(
            collective_id=1, has_side_effects=True, vmem_limit_bytes=VMEM_BYTES),
    )(*inputs.values())
    return fresh[:, None], hess[:, 0, :base_count + ITERS + 1]


def solution(mesh):
    return jax.shard_map(
        per_device,
        mesh=mesh,
        in_specs=(
            P(None, "replica", None),
            P("section", None, None),
            P("section", None, None),
            P("section", None),
            P(None, "section", None, "replica", None),
        ),
        out_specs=(P(None, "section", None, "replica", None), P()),
        check_vma=False,
    )
```

time: 1240 us -> 239 us (0.19)
  waiting for transfers between devices: 569 us -> 0 us
  blocking collectives: 453 us -> 0 us
  Pallas kernels: 0 us -> 236 us
  matrix products: 86.5 us -> 0 us
  starting transfers between devices: 57.4 us -> 0 us
  other arithmetic: 30.5 us -> 0 us
  local copies, waits for them, and re-layouts: 19.7 us -> 2.83 us
  between operations: 17.1 us -> 0.64 us
    psum x6 -> x0, blocking collectives: 453 us -> none  [the longest x2 159 us: per_device(): lax.psum(local_correlations(slot_bank, image), ('section', 'replica'))]
    reduce_scatter x2 -> x0, waiting for transfers between devices: 284 us -> none  [curvature_product(): lax.psum_scatter(term_sum, 'replica', scatter_dimension=2, tiled=True)]
    pallas_call x0 -> x1, Pallas kernels: none -> 236 us  [per_device(): pl.pallas_call(functools.partial(main_kernel, cfg, names), out_shape=tupl...]
    all_gather x2 -> x0, waiting for transfers between devices: 148 us -> none  [curvature_product(): tangent_full = lax.all_gather(tangent_shard, 'replica', axis=2, tiled=True)]
    ppermute x20 -> x0, waiting for transfers between devices: 137 us -> none  [shifted(): return lax.ppermute(block, axis, route)]
    dot_general x69 -> x0, matrix products: 86.5 us -> none  [the longest x32 64.6 us: against_rows(): lax.dot_general(left, right, (((1,), (1,)), ((), ())), preferred_element_...]
    ppermute x20 -> x0, starting transfers between devices: 57.2 us -> none  [shifted(): return lax.ppermute(block, axis, route)]
  transfers between devices with their start and end apart: 24 -> 0, of which waited for: 20 -> 0; matrix products, arithmetic and copies ran while one was open for 4% -> 0% of each run, Pallas kernels for 0% -> 0%
where the time goes in v1:
time: 239 us
  Pallas kernels  236 us (99%)
  local copies, waits for them, and re-layouts  2.83 us (1%)
    pallas_call x1, Pallas kernels, per_device(): pl.pallas_call(functools.partial(main_kernel, cfg, names), out_shape=tupl...  236 us

profile of v1, /device:TPU:1, one launch (start us, length us, event | category | flops | bytes accessed | tf_op | source)
XLA Modules:
  0.0 239.2 jit_solution(12522818528805740547)
XLA Ops:
  0.6 235.7 %shard_map.68 = (f32[2,2,64,128]{3,2,1,0:T(8,128)}, f32[2,8,128]{2,1,0:T(8,128)}) custom-call(bf16[128,4096]{1,0:T(8,128)(2,1)} %bitcast.8, bf16[4,8,2,64,128]{4,3,2,1,0:T(8,128)(2,1)} %bitcast.9, bf16[4,8,2,64,128]{4,3,2,1,0:T(8,128)(2,1)} %bitcast.10, f32[1,4096]{1,0:T(1,128)} %refs_3_.1, f32[6,2,64,128]{3,2,1,0:T(8,128)} %bitcast.11), custom_call_target="tpu_custom_call" | custom-call | tf_op jit(solution)/shard_map/pallas_call | solution.py:955
  236.3 1.3 slice.3
  237.6 1.6 copy.9

commit v2 on v1

--- a/solution.py
+++ b/solution.py
@@ -19,6 +19,7 @@
 BF16 = jnp.bfloat16
 VMEM_BYTES = 56 * 1024 * 1024
 Y_CHUNKS = 2
+ROWS_A = 64
 
 
 def dot(left, right):
@@ -144,9 +145,9 @@
 def gather_sems(blocks):
     first = blocks // 2
     dma = pltpu.SemaphoreType.DMA
-    ring = (2 * ZS, first)
-    return [dma((YS - 1,)), dma((YS - 1,)), dma(ring), dma(ring), dma(ring), dma(ring),
-            dma((2 * ZS,)), dma((2 * ZS,)), dma((YS,)), dma((YS,)), dma((YS,)), dma((YS,))]
+    ring, hand = (ZS - 1, first), (ZS, first)
+    return [dma((YS - 1,)), dma((YS - 1,)), dma(ring), dma(ring), dma(hand), dma(hand),
+            dma((ZS - 1,)), dma((ZS - 1,)), dma((YS,)), dma((YS,)), dma((YS,)), dma((YS,))]
 
 
 def ring_steps():
@@ -161,8 +162,13 @@
     def bundle(chunk, z, core):
         return out.at[blocks[chunk], :, z, core]
 
+    steps = ring_steps()
+
     def index(step, way):
-        return 2 * step + (way > 0)
+        return steps.index((step, way))
+
+    def hand_index(step, way):
+        return 0 if step == 0 else index(step, way) + 1
 
     def send(step, way, chunk):
         view = bundle(chunk, at.z_at(-way * (step - 1)), at.core)
@@ -173,8 +179,8 @@
 
     def hand_on(step, way, chunk):
         view = bundle(chunk, at.z_at(-way * step), at.core)
-        copy = remote(view, view, csend.at[index(step, way), chunk], crecv.at[index(step, way), chunk],
-                      at.sibling)
+        copy = remote(view, view, csend.at[hand_index(step, way), chunk],
+                      crecv.at[hand_index(step, way), chunk], at.sibling)
         copy.start()
         sends.append(copy)
 
@@ -187,7 +193,6 @@
         send(1, -1, chunk)
     for chunk in range(len(blocks)):
         hand_on(0, 1, chunk)
-    steps = ring_steps()
     for step in range(1, HALF + 1):
         for chunk in range(len(blocks)):
             yield
@@ -204,25 +209,16 @@
         yield
         for chunk in range(len(blocks)):
             view = bundle(chunk, at.z_at(-way * step), 1 - at.core)
-            remote(view, view, csend.at[index(step, way), chunk], crecv.at[index(step, way), chunk],
-                   at.sibling).wait_recv()
-
-
-def gather_second(out, blocks, at, sems, sends):
+            remote(view, view, csend.at[hand_index(step, way), chunk],
+                   crecv.at[hand_index(step, way), chunk], at.sibling).wait_recv()
+
+
+def gather_second(out, blocks, at, sems, sends, pauses):
     zsend, zrecv, ysend, yrecv, csend, crecv = sems
     span = pl.ds(blocks[0], len(blocks))
 
     def view(z):
         return out.at[span, at.why, z, at.core]
-
-    def index(step, way):
-        return 2 * step + (way > 0)
-
-    def send(step, way):
-        block = view(at.z_at(-way * (step - 1)))
-        copy = remote(block, block, zsend.at[index(step, way)], zrecv.at[index(step, way)], at.z(way))
-        copy.start()
-        sends.append(copy)
 
     def bundle(step, core, part=None):
         zeds = pl.ds(0, ZS) if part is None else pl.ds(part * HALF, HALF)
@@ -239,30 +235,24 @@
         copy.start()
         sends.append(copy)
 
-    send(1, 1)
-    send(1, -1)
-    steps = ring_steps()
-    for step in range(1, HALF + 1):
+    exchange(sends, ZS, at.z, lambda step: view(at.zed), lambda step: view(at.zed), zsend, zrecv)
+    for _ in range(pauses[0]):
         yield
-        for way in (1, -1):
-            if (step, way) not in steps:
-                continue
-            block = view(at.z_at(-way * step))
-            remote(block, block, zsend.at[index(step, way)], zrecv.at[index(step, way)],
-                   at.sibling).wait_recv()
-            if (step + 1, way) in steps:
-                send(step + 1, way)
+    for step in range(1, ZS):
+        arrived(view(at.z_at(-step)), zsend, zrecv, step - 1, at.sibling)
     along(bundle(0, at.core), 0, 1)
     along(bundle(0, at.core), 1, -1)
     hand_on(0, 0)
-    yield
+    for _ in range(pauses[1]):
+        yield
     arrived(bundle(-1, at.core), ysend, yrecv, 0, at.sibling)
     along(bundle(-1, at.core, 0), 2, 1)
     arrived(bundle(1, at.core), ysend, yrecv, 1, at.sibling)
     along(bundle(1, at.core, 1), 3, -1)
     hand_on(-1, 1)
     hand_on(1, 2)
-    yield
+    for _ in range(pauses[2]):
+        yield
     arrived(bundle(2, at.core, 0), ysend, yrecv, 2, at.sibling)
     arrived(bundle(2, at.core, 1), ysend, yrecv, 3, at.sibling)
     hand_on(2, 3)
@@ -275,7 +265,9 @@
     half = count // 2
     first = list(range(start, start + half))
     second = list(range(start + half, start + count))
-    return merged(gather_second(out, second, at, sems[6:], sends),
+    chunks = len(first)
+    pauses = (chunks + 2, 2 * chunks - 1, chunks)
+    return merged(gather_second(out, second, at, sems[6:], sends, pauses),
                   gather_first(out, first, at, sems[:6], sends))
 
 
@@ -285,11 +277,20 @@
     return wide.reshape(TILE, 128)
 
 
-def tiles(full_d, body):
+def tiles(full_d, body, between=None, parts=1):
     def step(idx, carry):
         body(idx, pl.ds(pl.multiple_of(idx * TILE, TILE), TILE))
         return carry
-    lax.fori_loop(0, full_d // TILE, step, 0)
+    count = full_d // TILE // parts
+    for part in range(parts):
+        lax.fori_loop(part * count, (part + 1) * count, step, 0)
+        if between is not None:
+            between()
+
+
+def every_up(ref, at, idx):
+    return jnp.concatenate(
+        [row_block(ref.weights, 2 * at.slot(layer) + 1, idx) for layer in range(at.layers)], axis=1)
 
 
 def lane_sums(wide):
@@ -299,20 +300,16 @@
 def primal(ref, at, full_d, between):
     layers, sec = at.layers, at.sec
     tokens = ref.rows.shape[0]
-    part = tokens // layers
     acc, along = ref.acc, ref.along
-    mine = pl.ds(pl.multiple_of(sec * part, part), part)
     along[0] = jnp.zeros((tokens, 128), F32)
 
-    def rows_of(layer, where, cols):
-        return ref.rows[where, cols] if layer == 0 else ref.every_row[layer - 1, where, cols]
-
-    everywhere = slice(None)
+    def rows_of(layer, cols):
+        return ref.rows[:, cols] if layer == 0 else ref.every_row[layer - 1, :, cols]
 
     def square(idx, cols):
         wide = ref.rows[:, cols].astype(F32)
         along[0] += lane_sums(wide * wide)
-    tiles(full_d, square)
+    tiles(full_d, square, between)
     for layer in range(layers):
         down, up = 2 * at.slot(layer), 2 * at.slot(layer) + 1
         mean = jnp.sum(along[0], axis=-1, keepdims=True) * (1.0 / full_d)
@@ -321,14 +318,13 @@
 
         def project(idx, cols):
             gain = ref.gains[at.slot(layer), :, cols]
-            piece = (rows_of(layer, everywhere, cols).astype(F32) * inv * gain).astype(BF16)
+            piece = (rows_of(layer, cols).astype(F32) * inv * gain).astype(BF16)
 
             @pl.when(sec == layer)
             def _():
                 ref.normed[:, cols] = piece
             acc[0] += dot(piece, row_block(ref.weights, down, idx))
-        tiles(full_d, project)
-        between()
+        tiles(full_d, project, between, 2)
         pre = acc[0]
         sig = jax.nn.sigmoid(pre)
         act = (pre * sig).astype(BF16)
@@ -343,21 +339,27 @@
         along[0] = jnp.zeros((tokens, 128), F32)
         if layer + 1 < layers:
             def forward(idx, cols):
-                wide = rows_of(layer, everywhere, cols).astype(F32)
+                wide = rows_of(layer, cols).astype(F32)
                 wide = wide + dot_t(act, row_block(ref.weights, up, idx))
                 rounded = wide.astype(BF16)
                 ref.every_row[layer, :, cols] = rounded
                 again = rounded.astype(F32)
                 along[0] += lane_sums(again * again)
-            tiles(full_d, forward)
-            between()
+            tiles(full_d, forward, between, 2)
+    ref.gram[...] = over_tokens(ref.hidden[...], ref.own_hidden[...])
+    between()
+
+
+def weight_products(ref, at, full_d, between):
+    layers, sec = at.layers, at.sec
+    part = ref.rows.shape[0] // layers
+    mine = pl.ds(pl.multiple_of(sec * part, part), part)
     ref.uu[...] = jnp.zeros_like(ref.uu)
     ref.ud[...] = jnp.zeros_like(ref.ud)
     ref.row_up[...] = jnp.zeros_like(ref.row_up)
 
     def grams(idx, cols):
-        ups = [row_block(ref.weights, 2 * at.slot(layer) + 1, idx) for layer in range(layers)]
-        every = jnp.concatenate(ups, axis=1)
+        every = every_up(ref, at, idx)
         turned = every.T
         ref.uu[...] += dot(turned, every)
         pair_at = 0
@@ -367,16 +369,14 @@
             high, low = two_parts(turned[:width].astype(F32) * gain)
             down = row_block(ref.weights, 2 * at.slot(layer), idx)
             pair = dot(high, down) + dot(low, down)
-            block = dot(rows_of(layer, mine, cols), every[:, :width])
+            block = dot(ref.every_row[layer - 1, mine, cols], every[:, :width])
             for k in range(layer):
                 ref.ud[pair_at] += pair[k * 128:(k + 1) * 128]
                 ref.row_up[pair_at] += block[:, k * 128:(k + 1) * 128]
                 pair_at += 1
-    tiles(full_d, grams)
-    between()
+    tiles(full_d, grams, between, 4)
     ref.uu_high[...], ref.uu_low[...] = two_parts(ref.uu[...])
     ref.ud_high[...], ref.ud_low[...] = two_parts(ref.ud[...])
-    ref.gram[...] = over_tokens(ref.hidden[...], ref.own_hidden[...])
 
 
 def recurrence(tan_base, back_base, pre_act, slope, inv_rms, row_up, up_up, up_down, full_d):
@@ -414,6 +414,7 @@
     layers, sec = at.layers, at.sec
     acc, along = ref.acc, ref.along
     acc[...] = jnp.zeros_like(acc)
+    ref.acc_up[...] = jnp.zeros_like(ref.acc_up)
     along[...] = jnp.zeros_like(along)
     own_hidden = ref.own_hidden[...]
     part = own_hidden.shape[0] // layers
@@ -422,8 +423,7 @@
         acc[0] += dot(ref.normed[:, cols], row_block(ref.vector, 0, idx))
         spread = dot_t(own_hidden, row_block(ref.vector, 1, idx))
         rounded = spread.astype(BF16)
-        for layer in range(layers):
-            acc[layers + layer] += dot(rounded, row_block(ref.weights, 2 * at.slot(layer) + 1, idx))
+        ref.acc_up[...] += dot(rounded, every_up(ref, at, idx))
         for layer in range(1, layers):
             scaled = (spread * ref.gains[at.slot(layer), :, cols]).astype(BF16)
             acc[layer] += dot(scaled, row_block(ref.weights, 2 * at.slot(layer), idx))
@@ -443,7 +443,7 @@
             later = inv * acc[layer] - (inv * inv * (1.0 / full_d)) * reach * ref.pre_act[layer]
             own = own + jnp.where(sec < layer, later, 0.0)
         put(layer, own)
-        put(layers + layer, acc[layers + layer])
+        put(layers + layer, ref.acc_up[:, layer * 128:(layer + 1) * 128])
 
 
 def gradient_terms(ref, at, full_d):
@@ -469,6 +469,7 @@
         acts.insert(0, (column(layer).astype(F32) - later * old).astype(BF16))
         later = later + pulls[layer]
     total = later[:, :1]
+    act_cat = jnp.concatenate(acts, axis=1)
     own_back = back[0]
     for layer in range(1, layers):
         own_back = jnp.where(sec == layer, back[layer], own_back)
@@ -476,30 +477,23 @@
     per = TILE // (CS * 64)
 
     def body(idx, cols):
-        cot = -total * ref.rows[:, cols].astype(F32)
-        for layer in range(layers):
-            cot = cot + dot_t(acts[layer], row_block(ref.weights, 2 * at.slot(layer) + 1, idx))
+        cot = dot_t(act_cat, every_up(ref, at, idx)) - total * ref.rows[:, cols].astype(F32)
         for layer in range(1, layers):
             cot = cot + (dot_t(moved[layer], row_block(ref.weights, 2 * at.slot(layer), idx))
                          * ref.gains[at.slot(layer), :, cols])
         where = (idx // (ZS // per), pl.ds((idx % (ZS // per)) * per, per))
-        ref.part_b[where] = over_tokens(cot.astype(BF16), own_hidden).reshape(per, CS, 64, 128)
-        ref.part_a[where] = over_tokens(ref.normed[:, cols], own_back).reshape(per, CS, 64, 128)
-        for copy in swap_copies(ref, at, idx):
-            copy.start()
+        up = over_tokens(cot.astype(BF16), own_hidden).reshape(per, CS, 64, 128)
+        down = over_tokens(ref.normed[:, cols], own_back).reshape(per, CS, 64, 128)
+        ref.part[where] = jnp.concatenate([down, up], axis=2)
+        swap_copy(ref, at, idx).start()
     tiles(full_d, body)
 
 
-def swap_copies(ref, at, idx):
+def swap_copy(ref, at, idx):
     per = TILE // (CS * 64)
     where = (idx // (ZS // per), pl.ds((idx % (ZS // per)) * per, per))
-    other = where + (1 - at.core,)
-    return (
-        remote(ref.part_b.at[other], ref.swap_b.at[where], ref.swap_send.at[0, idx], ref.swap_recv.at[0, idx],
-               at.sibling),
-        remote(ref.part_a.at[other], ref.swap_a.at[where], ref.swap_send.at[1, idx], ref.swap_recv.at[1, idx],
-               at.sibling),
-    )
+    return remote(ref.part.at[where + (1 - at.core,)], ref.swap.at[where], ref.swap_send.at[idx],
+                  ref.swap_recv.at[idx], at.sibling)
 
 
 def scatter_first(ref, at, sends, done):
@@ -511,7 +505,7 @@
 
     def chip_sum(z, chunk):
         span = chunk_of(chunk)
-        return ref.swap_a[span, z] + ref.part_a[span, z, at.core]
+        return ref.swap[span, z, :ROWS_A] + ref.part[span, z, at.core, :ROWS_A]
 
     def left(step, chunk):
         z = at.z_at(step - HALF - 1)
@@ -572,7 +566,7 @@
 
     def chip_sum(step, half):
         y = at.y_at(step)
-        return ref.swap_b[y, halves[half]] + ref.part_b[y, halves[half], at.core]
+        return ref.swap[y, halves[half], ROWS_A:] + ref.part[y, halves[half], at.core, ROWS_A:]
 
     def go(src, dst, idx, way):
         copy = remote(src, dst, ref.ybs.at[idx], ref.ybr.at[idx], at.y(way))
@@ -593,6 +587,7 @@
     go(view(1, 1), ref.from_low.at[halves[1]], 2, 1)
     out[at.y_at(-1), halves[0]] = chip_sum(-1, 0)
     go(view(-1, 0), ref.from_high.at[halves[0]], 3, -1)
+    yield
     yield
     took(ref.chain.at[0], 0)
     out[at.y_at(1), halves[0]] = chip_sum(1, 0) + ref.chain[0]
@@ -624,12 +619,13 @@
 
 def scatter_sum(ref, at, full_d, sends):
     for idx in range(full_d // TILE):
-        for copy in swap_copies(ref, at, idx):
-            copy.wait_recv()
-            sends.append(copy)
+        copy = swap_copy(ref, at, idx)
+        copy.wait_recv()
+        sends.append(copy)
     done_a, done_b = [], []
     finish(merged(scatter_second(ref, at, sends, done_b), scatter_first(ref, at, sends, done_a)))
-    return done_a[0], done_b[0]
+    both = jnp.concatenate([done_a[0], done_b[0]], axis=0)
+    return both[:64], both[64:]
 
 
 def gram_steps(ref, at, sends):
@@ -778,11 +774,16 @@
         copy.wait()
     moving = gather(ref.vector, 0, 2, at, sems[GATHER_KINDS:], sends)
 
+    calls = []
+
     def move():
-        next(moving, None)
-        next(moving, None)
-    move()
+        calls.append(None)
+        if len(calls) % 2 == 0:
+            next(moving, None)
+    next(moving, None)
+    next(moving, None)
     primal(ref, at, full_d, move)
+    weight_products(ref, at, full_d, move)
     finish(moving)
     ups_arrived(ref, at)
     drain(sends)
@@ -844,7 +845,7 @@
         for k in range(count):
             line = jnp.where(lane == k, coef[k], line)
         line = jnp.where(lane == base_count + ITERS, length, line)
-        ref.hess[it] = jnp.broadcast_to(line, (8, 128))
+        ref.hess[it:it + 1, :] = line[:, :base_count + ITERS + 1]
         drain(sends)
         if it + 1 < ITERS:
             held.append((ref.fresh[it, 0], ref.fresh[it, 1]))
@@ -870,6 +871,7 @@
     pairs = layers * (layers - 1) // 2
     wide = layers * rank
     piece = wide // inner
+    rows_b = 2 * rows - ROWS_A
 
     inputs = dict(
         rows=hidden_in.reshape(tokens, full_d),
@@ -880,7 +882,7 @@
     )
     outputs = dict(
         fresh=jax.ShapeDtypeStruct((ITERS, 2, rows, rank), F32),
-        hess=jax.ShapeDtypeStruct((ITERS, 8, 128), F32),
+        hess=jax.ShapeDtypeStruct((ITERS, base_count + ITERS + 1), F32),
     )
     scratch = dict(
         weights=pltpu.VMEM((2 * layers,) + split, BF16),
@@ -908,24 +910,23 @@
         gram_sum=pltpu.VMEM((piece, rank), F32),
         gram_in2=pltpu.VMEM((YS - 1, piece // YS, rank), F32),
         gram_out=pltpu.VMEM((piece, rank), F32),
-        acc=pltpu.VMEM((2 * layers, tokens, rank), F32),
+        acc=pltpu.VMEM((layers, tokens, rank), F32),
+        acc_up=pltpu.VMEM((tokens, wide), F32),
         along=pltpu.VMEM((layers, tokens, 128), F32),
         pay=pltpu.VMEM((layers, part, 2 * wide), BF16),
         pay_in=pltpu.VMEM((layers - 1, part, 2 * wide), BF16),
         result=pltpu.VMEM((layers, part, 2 * wide), BF16),
-        part_a=pltpu.VMEM(split, F32),
-        part_b=pltpu.VMEM(split, F32),
-        swap_a=pltpu.VMEM((YS, ZS, rows, rank), F32),
-        swap_b=pltpu.VMEM((YS, ZS, rows, rank), F32),
-        out_a=pltpu.VMEM((YS, ZS, rows, rank), F32),
-        out_b=pltpu.VMEM((YS, ZS, rows, rank), F32),
-        left_in=pltpu.VMEM((HALF, YS, rows, rank), F32),
-        right_in=pltpu.VMEM((HALF - 1, YS, rows, rank), F32),
-        y_a=pltpu.VMEM((YS - 1, rows, rank), F32),
-        chain=pltpu.VMEM((2, HALF, rows, rank), F32),
-        from_low=pltpu.VMEM((ZS, rows, rank), F32),
-        from_high=pltpu.VMEM((ZS, rows, rank), F32),
-        z_b=pltpu.VMEM((ZS - 1, rows, rank), F32),
+        part=pltpu.VMEM((YS, ZS, CS, 2 * rows, rank), F32),
+        swap=pltpu.VMEM((YS, ZS, 2 * rows, rank), F32),
+        out_a=pltpu.VMEM((YS, ZS, ROWS_A, rank), F32),
+        out_b=pltpu.VMEM((YS, ZS, rows_b, rank), F32),
+        left_in=pltpu.VMEM((HALF, YS, ROWS_A, rank), F32),
+        right_in=pltpu.VMEM((HALF - 1, YS, ROWS_A, rank), F32),
+        y_a=pltpu.VMEM((YS - 1, ROWS_A, rank), F32),
+        chain=pltpu.VMEM((2, HALF, rows_b, rank), F32),
+        from_low=pltpu.VMEM((ZS, rows_b, rank), F32),
+        from_high=pltpu.VMEM((ZS, rows_b, rank), F32),
+        z_b=pltpu.VMEM((ZS - 1, rows_b, rank), F32),
         vec=pltpu.VMEM((8, 128), F32),
         near=pltpu.VMEM((inner, 8, 128), F32),
         far=pltpu.VMEM((outer, 8, 128), F32),
@@ -940,7 +941,7 @@
         g2s=dma((YS - 1,)), g2r=dma((YS - 1,)),
         g3s=dma((YS - 1,)), g3r=dma((YS - 1,)),
         g4s=dma((inner - 1,)), g4r=dma((inner - 1,)),
-        swap_send=dma((2, full_d // TILE)), swap_recv=dma((2, full_d // TILE)),
+        swap_send=dma((full_d // TILE,)), swap_recv=dma((full_d // TILE,)),
         ls=dma((HALF, Y_CHUNKS)), lr=dma((HALF, Y_CHUNKS)),
         rs=dma((HALF - 1, Y_CHUNKS)), rr=dma((HALF - 1, Y_CHUNKS)),
         yas=dma((YS - 1,)), yar=dma((YS - 1,)),
@@ -961,7 +962,7 @@
         compiler_params=pltpu.CompilerParams(
             collective_id=1, has_side_effects=True, vmem_limit_bytes=VMEM_BYTES),
     )(*inputs.values())
-    return fresh[:, None], hess[:, 0, :base_count + ITERS + 1]
+    return fresh[:, None], hess
 
 
 def solution(mesh):

time: 239 us -> 216 us (0.904)
  Pallas kernels: 236 us -> 213 us
    pallas_call x1, Pallas kernels: 236 us -> 213 us  [per_device(): pl.pallas_call(functools.partial(main_kernel, cfg, names), out_shape=tupl...]
where the time goes in v2:
time: 216 us
  Pallas kernels  213 us (99%)
    pallas_call x1, Pallas kernels, per_device(): pl.pallas_call(functools.partial(main_kernel, cfg, names), out_shape=tupl...  213 us

profile of v2, /device:TPU:1, one launch (start us, length us, event | category | flops | bytes accessed | tf_op | source)
XLA Modules:
  0.0 216.0 jit_solution(9084868099680988475)
XLA Ops:
  0.6 213.2 %shard_map.68 = (f32[2,2,64,128]{3,2,1,0:T(8,128)}, f32[2,9]{1,0:T(2,128)}) custom-call(bf16[128,4096]{1,0:T(8,128)(2,1)} %bitcast.7, bf16[4,8,2,64,128]{4,3,2,1,0:T(8,128)(2,1)} %bitcast.8, bf16[4,8,2,64,128]{4,3,2,1,0:T(8,128)(2,1)} %bitcast.9, f32[1,4096]{1,0:T(1,128)} %refs_3_.1, f32[6,2,64,128]{3,2,1,0:T(8,128)} %bitcast.10), custom_call_target="tpu_custom_call" | custom-call | tf_op jit(solution)/shard_map/pallas_call | solution.py:956
  213.9 0.0 copy-start
  213.9 1.6 copy.10
  215.5 0.0 copy-done
  215.5 0.6 copy.11
Async XLA Ops:
  213.9 1.6 copy-start

commit v3 on v2

--- a/solution.py
+++ b/solution.py
@@ -266,7 +266,7 @@
     first = list(range(start, start + half))
     second = list(range(start + half, start + count))
     chunks = len(first)
-    pauses = (chunks + 2, 2 * chunks - 1, chunks)
+    pauses = (chunks + 1, 2 * chunks, chunks + 1)
     return merged(gather_second(out, second, at, sems[6:], sends, pauses),
                   gather_first(out, first, at, sems[:6], sends))
 

time: 216 us -> 214 us (level)
    pallas_call x1, Pallas kernels: 213 us -> 211 us  [per_device(): pl.pallas_call(functools.partial(main_kernel, cfg, names), out_shape=tupl...]
where the time goes in v3:
time: 214 us
  Pallas kernels  211 us (99%)
  local copies, waits for them, and re-layouts  2.14 us (1%)
    pallas_call x1, Pallas kernels, per_device(): pl.pallas_call(functools.partial(main_kernel, cfg, names), out_shape=tupl...  211 us

profile of v3, /device:TPU:1, one launch (start us, length us, event | category | flops | bytes accessed | tf_op | source)
XLA Modules:
  0.0 213.8 jit_solution(9268791304276540882)
XLA Ops:
  0.6 211.0 %shard_map.68 = (f32[2,2,64,128]{3,2,1,0:T(8,128)}, f32[2,9]{1,0:T(2,128)}) custom-call(bf16[128,4096]{1,0:T(8,128)(2,1)} %bitcast.7, bf16[4,8,2,64,128]{4,3,2,1,0:T(8,128)(2,1)} %bitcast.8, bf16[4,8,2,64,128]{4,3,2,1,0:T(8,128)(2,1)} %bitcast.9, f32[1,4096]{1,0:T(1,128)} %refs_3_.1, f32[6,2,64,128]{3,2,1,0:T(8,128)} %bitcast.10), custom_call_target="tpu_custom_call" | custom-call | tf_op jit(solution)/shard_map/pallas_call | solution.py:956
  211.6 0.0 copy-start
  211.6 1.6 copy.10
  213.2 0.0 copy-done
  213.2 0.6 copy.11
Async XLA Ops:
  211.6 1.6 copy-start
